TPU v7x, 32 devices: a whole 2x2x4 slice. The times are simulated.
32 devices in a mesh: dp: 8 (over z, y), mp: 4 (over x, core).
Axes of the slice: x: 2, y: 2, z: 4, core: 2. Of those that a mesh axis runs over, the one named last changes fastest.
Arguments:
- block_input: bfloat16 [16384, 512], P(('dp', 'mp')), may hold values from -6 to 6
- memory: bfloat16 [32, 512, 512], P('dp', 'mp'), may hold values from -6 to 6
- cotangent: bfloat16 [16384, 512], P(('dp', 'mp')), may hold values from -6 to 6
- neighbour_table: bfloat16 [32768, 512], P('dp'), may hold values from -6 to 6
- requests: int32 [256, 256], P(('dp', 'mp')), may hold values from 0 to 4095, as said below
- counts: int32 [256], P(('dp', 'mp')), may hold values from 128 to 256, as said below
- neighbour_slots: int32 [16384, 4], P(('dp', 'mp')), may hold values from 0 to 2047, as said below
- memory_lengths: int32 [32], P('dp'), may hold values from 0 to 512
- document_lengths: int32 [32], P('dp'), may hold values from 1 to 512, as said below
- first_gain: float32 [512], replicated, may hold values from 0.5 to 1.5
- first_bias: float32 [512], replicated, may hold values from -1.75 to 1.75
- query_weight: bfloat16 [512, 512], P(None, 'mp'), may hold values from -0.25 to 0.25
- key_weight: bfloat16 [512, 512], P(None, 'mp'), may hold values from -0.25 to 0.25
- value_weight: bfloat16 [512, 512], P(None, 'mp'), may hold values from -0.25 to 0.25
- position_weight: bfloat16 [512, 512], P(None, 'mp'), may hold values from -0.25 to 0.25
- content_bias: float32 [512], P('mp'), may hold values from -3 to 3
- position_bias: float32 [512], P('mp'), may hold values from -3 to 3
- output_weight: bfloat16 [512, 512], P('mp'), may hold values from -2 to 2
- second_gain: float32 [512], replicated, may hold values from 0.5 to 1.5
- second_bias: float32 [512], replicated, may hold values from -1.75 to 1.75
- inner_weight: bfloat16 [512, 2048], P(None, 'mp'), may hold values from -0.25 to 0.25
- inner_bias: bfloat16 [2048], P('mp'), may hold values from -3 to 3
- outer_weight: bfloat16 [2048, 512], P('mp'), may hold values from -0.125 to 0.125
- outer_bias: float32 [512], replicated, may hold values from -1.75 to 1.75
- gate_weight: float32 [512], replicated, may hold values from -0.25 to 0.25
Outputs:
- mixed_output: bfloat16 [16384, 512], P(('dp', 'mp'))
- input_grad: float32 [16384, 512], P(('dp', 'mp'))
- first_gain_grad: float32 [512], replicated
- first_bias_grad: float32 [512], replicated
- query_weight_grad: float32 [512, 512], P(None, 'mp')
- key_weight_grad: float32 [512, 512], P(None, 'mp')
- value_weight_grad: float32 [512, 512], P(None, 'mp')
- position_weight_grad: float32 [512, 512], P(None, 'mp')
- content_bias_grad: float32 [512], P('mp')
- position_bias_grad: float32 [512], P('mp')
- output_weight_grad: float32 [512, 512], P('mp')
- second_gain_grad: float32 [512], replicated
- second_bias_grad: float32 [512], replicated
- inner_weight_grad: float32 [512, 2048], P(None, 'mp')
- inner_bias_grad: float32 [2048], P('mp')
- outer_weight_grad: float32 [2048, 512], P('mp')
- outer_bias_grad: float32 [512], replicated
- gate_weight_grad: float32 [512], replicated
Inputs may be any that keep to these rules, and one draw needn't show every extreme that they name: `neighbour_slots`: each entry is 256 * o + p for an owner o and a place p below the count of that owner's list on the token's device. `requests`: row numbers within the owner's shard of neighbour_table; entries at or past a list's count are filler. `counts`: every device has a list filled to 256, and one owner receives 256 entries from every device. `document_lengths`: in each index of dp one row is 512 long.
All inputs are finite; a program needn't handle non-finite values.
Results may differ from a plain program's by a relative error of at most 0.015.
Values may be sent and summed in bfloat16 or wider, within the bound.
No kernel may reach another device: no remote copies, remote signals or barrier semaphores. Data moves between devices by JAX's collectives and lax.ppermute only.
A program may use at most 192 MiB of HBM per device.

v0:
```python
import math

import jax
import jax.numpy as jnp
from jax import lax
from jax.sharding import PartitionSpec as P

D = 512
HD = 64
SEG = 512
MEM = 512
KEYS = 1024


epsilon = 1e-05
highest = lax.Precision.HIGHEST


def norm_rows(values, gains, offsets):
    average = jnp.mean(values, axis=-1, keepdims=True)
    centred = values - average
    spread = jnp.mean(centred * centred, axis=-1, keepdims=True)
    return centred * lax.rsqrt(spread + epsilon) * gains + offsets


def position_table():
    distance = (KEYS - 1 - jnp.arange(KEYS, dtype=jnp.int32)).astype(jnp.float32)
    exponent = jnp.arange(0, D, 2, dtype=jnp.int32).astype(jnp.float32) / D
    angles = distance[:, None] * jnp.exp(-math.log(10000.0) * exponent)[None, :]
    return jnp.concatenate([jnp.sin(angles), jnp.cos(angles)], axis=1)


def shift_rows(scores):
    leading = scores.shape[:-2]
    padding = [(0, 0)] * len(leading) + [(0, 0), (1, 0)]
    padded = jnp.pad(scores, padding)
    folded = padded.reshape(leading + (KEYS + 1, SEG))[..., 1:, :]
    return folded.reshape(leading + (SEG, KEYS))


def shift_back(grads):
    zeros_in = jnp.zeros(grads.shape, jnp.float32)
    return jax.vjp(shift_rows, zeros_in)[1](grads)[0]


def row_mask(memory_count, document_count):
    key_place = lax.broadcasted_iota(jnp.int32, (SEG, KEYS), 1)
    query_place = lax.broadcasted_iota(jnp.int32, (SEG, KEYS), 0)
    return (
        (key_place >= MEM - memory_count)
        & (key_place <= MEM + query_place)
        & (key_place < MEM + document_count)
    )


def mixing(hidden_state, nearby, gate_proj):
    relevance = jnp.einsum("td,tkd->tk", hidden_state, nearby, precision=highest) / math.sqrt(
        hidden_state.shape[-1]
    )
    attention = jax.nn.softmax(relevance, axis=-1)
    recalled = jnp.einsum("tk,tkd->td", attention, nearby, precision=highest)
    gating = jax.nn.sigmoid(jnp.dot(hidden_state, gate_proj, precision=highest))
    return hidden_state + gating[:, None] * (recalled - hidden_state)


def split_heads(rows):
    return rows.reshape(rows.shape[0], -1, HD)


def row_scores(content_q, position_q, key_rows, position_keys, memory_count, document_count):
    content = jnp.einsum(
        "qhe,khe->hqk",
        split_heads(content_q),
        split_heads(key_rows),
        preferred_element_type=jnp.float32,
    )
    position = shift_rows(
        jnp.einsum(
            "qhe,khe->hqk",
            split_heads(position_q),
            split_heads(position_keys),
            preferred_element_type=jnp.float32,
        )
    )
    scores = (content + position) * HD ** (-0.5)
    return jnp.where(row_mask(memory_count, document_count)[None], scores, -1e30)


def local(
    block_input,
    memory,
    cotangent,
    neighbour_table,
    requests,
    counts,
    neighbour_slots,
    memory_lengths,
    document_lengths,
    first_gain,
    first_bias,
    query_weight,
    key_weight,
    value_weight,
    position_weight,
    content_bias,
    position_bias,
    output_weight,
    second_gain,
    second_bias,
    inner_weight,
    inner_bias,
    outer_weight,
    outer_bias,
    gate_weight,
):
    model_size = lax.axis_size("mp")
    model_index = lax.axis_index("mp")
    local_tokens = block_input.shape[0]
    rows_group = memory_lengths.shape[0]
    rows_local = rows_group // model_size
    capacity = requests.shape[1]
    owners = requests.shape[0]
    found = jnp.take(
        neighbour_table,
        lax.all_to_all(requests, "dp", split_axis=0, concat_axis=0, tiled=True),
        axis=0,
    )
    fetched = lax.all_to_all(found, "dp", split_axis=0, concat_axis=0, tiled=True)
    live_slots = lax.broadcasted_iota(jnp.int32, (owners, capacity), 1) < counts[:, None]
    fetched = jnp.where(live_slots[:, :, None], fetched, jnp.zeros_like(fetched)).reshape(
        owners * capacity, D
    )
    nearby = jnp.take(fetched, neighbour_slots, axis=0).astype(jnp.float32)
    input_rows = block_input.astype(jnp.float32)
    local_docs = lax.dynamic_slice_in_dim(document_lengths, model_index * rows_local, rows_local)
    normed = norm_rows(input_rows, first_gain, first_bias).astype(jnp.bfloat16)
    memory_rows = memory.astype(jnp.float32)
    normed_memory = norm_rows(memory_rows, first_gain, first_bias).astype(jnp.bfloat16)
    normed_all, memory_all = (
        lax.all_gather(normed, "mp", axis=0, tiled=True),
        lax.all_gather(normed_memory, "mp", axis=1, tiled=True),
    )
    current = normed_all.reshape(rows_group, SEG, D)
    keys_in = jnp.concatenate([memory_all, current], axis=1)
    query_proj, key_proj, value_proj, place_proj = (
        query_weight,
        key_weight,
        value_weight,
        position_weight,
    )
    bias_content, bias_place, out_proj = (content_bias, position_bias, output_weight)
    query_rows = jnp.einsum("rqd,de->rqe", current, query_proj, preferred_element_type=jnp.float32)
    key_rows = jnp.einsum(
        "rkd,de->rke", keys_in, key_proj, preferred_element_type=jnp.float32
    ).astype(jnp.bfloat16)
    value_rows = jnp.einsum(
        "rkd,de->rke", keys_in, value_proj, preferred_element_type=jnp.float32
    ).astype(jnp.bfloat16)
    position_low = position_table().astype(jnp.bfloat16)
    position_keys = jnp.dot(position_low, place_proj, preferred_element_type=jnp.float32).astype(
        jnp.bfloat16
    )
    content_q = (query_rows + bias_content).astype(jnp.bfloat16)
    position_q = (query_rows + bias_place).astype(jnp.bfloat16)

    def attend(row_items):
        row_content, row_position, row_keys, row_values, memory_count, document_count = row_items
        scores = row_scores(
            row_content, row_position, row_keys, position_keys, memory_count, document_count
        )
        largest = jnp.max(scores, axis=-1, keepdims=True)
        raised = jnp.exp(scores - largest)
        total_weight = jnp.sum(raised, axis=-1, keepdims=True)
        softmaxed = (raised / total_weight).astype(jnp.bfloat16)
        result = jnp.einsum(
            "hqk,khe->qhe", softmaxed, split_heads(row_values), preferred_element_type=jnp.float32
        )
        return (result.reshape(SEG, -1), (largest + jnp.log(total_weight))[:, :, 0])

    attended, log_totals = lax.map(
        attend, (content_q, position_q, key_rows, value_rows, memory_lengths, document_lengths)
    )
    attended_low = attended.astype(jnp.bfloat16).reshape(rows_group * SEG, -1)
    middle = input_rows + lax.psum_scatter(
        jnp.dot(attended_low, out_proj, preferred_element_type=jnp.float32),
        "mp",
        scatter_dimension=0,
        tiled=True,
    )
    normed_middle = norm_rows(middle, second_gain, second_bias).astype(jnp.bfloat16)
    normed_full = lax.all_gather(normed_middle, "mp", axis=0, tiled=True)
    preact = jnp.dot(
        normed_full, inner_weight, preferred_element_type=jnp.float32
    ) + inner_bias.astype(jnp.float32)
    activation = jax.nn.gelu(preact).astype(jnp.bfloat16)
    outer_term = lax.psum_scatter(
        jnp.dot(activation, outer_weight, preferred_element_type=jnp.float32).astype(jnp.bfloat16),
        "mp",
        scatter_dimension=0,
        tiled=True,
    ).astype(jnp.float32)
    hidden = middle + outer_term + outer_bias

    def mix_local(hidden_state, gate_proj):
        return mixing(hidden_state, nearby, gate_proj)

    mixed, mixing_back = jax.vjp(mix_local, hidden, gate_weight)
    valid_tokens = (
        (lax.broadcasted_iota(jnp.int32, (rows_local, SEG), 1) < local_docs[:, None])
        .astype(jnp.float32)
        .reshape(local_tokens, 1)
    )
    grad_mixed = cotangent.astype(jnp.float32) * valid_tokens
    grad_hidden, grad_gate = mixing_back(grad_mixed)
    grad_outer_bias = jnp.sum(grad_hidden, axis=0)
    hidden_low = grad_hidden.astype(jnp.bfloat16)
    gelu_back = jax.vjp(jax.nn.gelu, preact)[1]
    grad_full = lax.all_gather(hidden_low, "mp", axis=0, tiled=True)
    grad_activation = jnp.einsum(
        "td,fd->tf", grad_full, outer_weight, preferred_element_type=jnp.float32
    )
    grad_preact = gelu_back(grad_activation)[0].astype(jnp.bfloat16)
    grad_inner = jnp.einsum(
        "td,tf->df", normed_full, grad_preact, preferred_element_type=jnp.float32
    )
    grad_inner_bias = jnp.sum(grad_preact.astype(jnp.float32), axis=0)
    grad_outer = jnp.einsum("tf,td->fd", activation, grad_full, preferred_element_type=jnp.float32)
    grad_normed_middle = lax.psum_scatter(
        jnp.einsum("tf,df->td", grad_preact, inner_weight, preferred_element_type=jnp.float32),
        "mp",
        scatter_dimension=0,
        tiled=True,
    )
    second_back = jax.vjp(norm_rows, middle, second_gain, second_bias)[1]
    grad_middle_norm, grad_second_gain, grad_second_bias = second_back(grad_normed_middle)
    grad_middle = grad_hidden + grad_middle_norm
    middle_low = grad_middle.astype(jnp.bfloat16)
    grad_attn_full = lax.all_gather(middle_low, "mp", axis=0, tiled=True)
    grad_output = jnp.einsum(
        "tc,td->cd", attended_low, grad_attn_full, preferred_element_type=jnp.float32
    )
    grad_attended = (
        jnp.einsum("td,cd->tc", grad_attn_full, out_proj, preferred_element_type=jnp.float32)
        .astype(jnp.bfloat16)
        .reshape(rows_group, SEG, -1)
    )

    def attend_back(row_items):
        (
            row_content,
            row_position,
            row_keys,
            row_values,
            memory_count,
            document_count,
            row_log,
            row_grad,
        ) = row_items
        scores = row_scores(
            row_content, row_position, row_keys, position_keys, memory_count, document_count
        )
        softmaxed = jnp.exp(scores - row_log[:, :, None])
        grad_heads = split_heads(row_grad)
        grad_soft = jnp.einsum(
            "qhe,khe->hqk", grad_heads, split_heads(row_values), preferred_element_type=jnp.float32
        )
        grad_values = jnp.einsum(
            "hqk,qhe->khe",
            softmaxed.astype(jnp.bfloat16),
            grad_heads,
            preferred_element_type=jnp.float32,
        )
        grad_scores = (
            softmaxed * (grad_soft - jnp.sum(softmaxed * grad_soft, axis=-1, keepdims=True))
        ).astype(jnp.bfloat16)
        grad_shifted = shift_back(grad_scores.astype(jnp.float32)).astype(jnp.bfloat16)
        score_scale = HD ** (-0.5)
        grad_content = score_scale * jnp.einsum(
            "hqk,khe->qhe", grad_scores, split_heads(row_keys), preferred_element_type=jnp.float32
        )
        grad_keys = score_scale * jnp.einsum(
            "hqk,qhe->khe",
            grad_scores,
            split_heads(row_content),
            preferred_element_type=jnp.float32,
        )
        grad_position = score_scale * jnp.einsum(
            "hqk,khe->qhe",
            grad_shifted,
            split_heads(position_keys),
            preferred_element_type=jnp.float32,
        )
        grad_table_keys = score_scale * jnp.einsum(
            "hqk,qhe->khe",
            grad_shifted,
            split_heads(row_position),
            preferred_element_type=jnp.float32,
        )
        return (
            grad_content.reshape(SEG, -1),
            grad_position.reshape(SEG, -1),
            grad_keys.reshape(KEYS, -1),
            grad_values.reshape(KEYS, -1),
            grad_table_keys.reshape(KEYS, -1),
        )

    grad_content, grad_position, grad_keys, grad_values, grad_table_keys = lax.map(
        attend_back,
        (
            content_q,
            position_q,
            key_rows,
            value_rows,
            memory_lengths,
            document_lengths,
            log_totals,
            grad_attended,
        ),
    )
    grad_query = (grad_content + grad_position).astype(jnp.bfloat16)
    grad_content_bias = jnp.sum(grad_content, axis=(0, 1))
    grad_position_bias = jnp.sum(grad_position, axis=(0, 1))
    keys_low = grad_keys.astype(jnp.bfloat16)
    values_low = grad_values.astype(jnp.bfloat16)
    grad_query_weight = jnp.einsum(
        "rqd,rqe->de", current, grad_query, preferred_element_type=jnp.float32
    )
    grad_key_weight = jnp.einsum(
        "rkd,rke->de", keys_in, keys_low, preferred_element_type=jnp.float32
    )
    grad_value_weight = jnp.einsum(
        "rkd,rke->de", keys_in, values_low, preferred_element_type=jnp.float32
    )
    grad_position_weight = jnp.einsum(
        "kd,ke->de",
        position_low.astype(jnp.float32),
        jnp.sum(grad_table_keys, axis=0),
        precision=highest,
    )
    grad_keys_in = jnp.einsum(
        "rke,de->rkd", keys_low, key_proj, preferred_element_type=jnp.float32
    ) + jnp.einsum("rke,de->rkd", values_low, value_proj, preferred_element_type=jnp.float32)
    grad_current = grad_keys_in[:, MEM:] + jnp.einsum(
        "rqe,de->rqd", grad_query, query_proj, preferred_element_type=jnp.float32
    )
    grad_normed, grad_normed_memory = (
        lax.psum_scatter(
            grad_current.reshape(rows_group * SEG, D).astype(jnp.bfloat16),
            "mp",
            scatter_dimension=0,
            tiled=True,
        ).astype(jnp.float32),
        lax.psum_scatter(
            grad_keys_in[:, :MEM].astype(jnp.bfloat16), "mp", scatter_dimension=1, tiled=True
        ).astype(jnp.float32),
    )
    first_back = jax.vjp(norm_rows, input_rows, first_gain, first_bias)[1]
    grad_input_norm, gain_from_input, bias_from_input = first_back(grad_normed)

    def memory_norm(gains, offsets):
        return norm_rows(memory_rows, gains, offsets)

    gain_from_memory, bias_from_memory = jax.vjp(memory_norm, first_gain, first_bias)[1](
        grad_normed_memory
    )
    input_grad = grad_middle + grad_input_norm
    summed = lax.psum(
        (
            grad_query_weight,
            grad_key_weight,
            grad_value_weight,
            grad_position_weight,
            grad_content_bias,
            grad_position_bias,
            grad_output,
            grad_inner,
            grad_inner_bias,
            grad_outer,
        ),
        "dp",
    )
    shared = lax.psum(
        (
            gain_from_input + gain_from_memory,
            bias_from_input + bias_from_memory,
            grad_second_gain,
            grad_second_bias,
            grad_outer_bias,
            grad_gate,
        ),
        ("dp", "mp"),
    )
    return (
        mixed.astype(jnp.bfloat16),
        input_grad,
        shared[0],
        shared[1],
        summed[0],
        summed[1],
        summed[2],
        summed[3],
        summed[4],
        summed[5],
        summed[6],
        shared[2],
        shared[3],
        summed[7],
        summed[8],
        summed[9],
        shared[4],
        shared[5],
    )


def solution(mesh):
    return jax.shard_map(
        local,
        mesh=mesh,
        in_specs=(
            P(("dp", "mp"), None),
            P("dp", "mp", None),
            P(("dp", "mp"), None),
            P("dp", None),
            P(("dp", "mp"), None),
            P(("dp", "mp")),
            P(("dp", "mp"), None),
            P("dp"),
            P("dp"),
            P(),
            P(),
            P(None, "mp"),
            P(None, "mp"),
            P(None, "mp"),
            P(None, "mp"),
            P("mp"),
            P("mp"),
            P("mp", None),
            P(),
            P(),
            P(None, "mp"),
            P("mp"),
            P("mp", None),
            P(),
            P(),
        ),
        out_specs=(
            P(("dp", "mp"), None),
            P(("dp", "mp"), None),
            P(),
            P(),
            P(None, "mp"),
            P(None, "mp"),
            P(None, "mp"),
            P(None, "mp"),
            P("mp"),
            P("mp"),
            P("mp", None),
            P(),
            P(),
            P(None, "mp"),
            P("mp"),
            P("mp", None),
            P(),
            P(),
        ),
        check_vma=False,
    )
```

profile of v0, /device:TPU:0, one launch (start us, length us, event | category | flops | bytes accessed | tf_op | source)
XLA Modules:
  0.0 985.6 jit_solution(12507012519026625386)
XLA Ops:
  21.5 17.1 %all-gather.8.cloned.1.call-done = bf16[2048,512]{1,0:T(8,128)(2,1)} async-done(((bf16[512,512]{1,0:T(8,128)(2,1)}), bf16[2048,512]{1,0:T(8,128)(2,1)}) %all-gather.8.cloned.1.call-update) | async-done | bytes 2097168 | tf_op jit(solution)/shard_map/all_gather | solution.py:140
  38.6 24.8 %all-gather.6.cloned.1.call-done = bf16[4,512,512]{2,1,0:T(8,128)(2,1)} async-done(((bf16[4,128,512]{2,1,0:T(8,128)(2,1)}), bf16[4,512,512]{2,1,0:T(8,128)(2,1)}) %all-gather.6.cloned.1.call-update) | async-done | bytes 2097168 | tf_op jit(solution)/shard_map/all_gather | solution.py:141
  76.7 136.8 %while.34 = (s32[]{:T(128)}, bf16[4,512,128]{2,1,0:T(8,128)(2,1)}, f32[4,2,512]{2,1,0:T(2,128)}, bf16[4,1024,128]{1,2,0:T(8,128)(2,1)}, s32[4]{0:T(128)S(1)}, /*...) while((s32[]{:T(128)}, bf16[4,512,128]{2,1,0:T(8,128)(2,1)}, ...), condition=%wide.region_7.8_spmd, body=%wide.region_4.7_spmd.sunk | while | flops 413664768 | bytes 58904784 | solution.py:180
  86.2 7.9 reshape.542
  98.8 5.3 reshape.543
  120.3 7.9 reshape.542
  128.2 4.7 slice.41
  132.9 5.3 reshape.543
  154.4 7.9 reshape.542
  167.0 5.3 reshape.543
  188.6 7.9 reshape.542
  196.4 4.7 slice.41
  201.1 5.3 reshape.543
  217.7 44.6 %reduce-scatter.6.cloned.1.call-done = f32[512,512]{1,0:T(8,128)} async-done(((f32[2048,512]{1,0:T(8,128)}), f32[512,512]{1,0:T(8,128)}) %reduce-scatter.6.cloned.1.call-update) | async-done | bytes 1048592 | tf_op jit(solution)/shard_map/reduce_scatter | solution.py:184
  266.3 5.5 all-to-all-start
  272.0 6.4 all-to-all-done
  278.4 10.9 %gather_fusion = bf16[2048,512]{1,0:T(8,128)(2,1)S(1)} fusion(bf16[4096,512]{1,0:T(8,128)(2,1)} %param.32, s32[2048]{0:T(1024)S(1)} %broadcast_clamp_fusion.1), kind=kCustom, calls=%fused_computation | custom fusion | bytes 4202496 | tf_op jit(solution)/shard_map/jit(_take)/gather | solution.py:123
  289.4 5.8 multiply_convert_fusion.1
  300.7 4.8 all-to-all-start.1
  308.0 46.2 %all-to-all-done.1 = bf16[8,256,512]{2,1,0:T(8,128)(2,1)} async-done(((bf16[8,256,512]{2,1,0:T(8,128)(2,1)}), bf16[8,256,512]{2,1,0:T(8,128)(2,1)}, u32[]{:S(2)}, u32[]{:S(2)}) %all-to-all-start.1) | async-done | bytes 2097184 | tf_op jit(solution)/shard_map/all_to_all | solution.py:128
  356.0 9.2 gather_fusion.1
  371.1 8.3 fusion.50
  382.7 5.5 fusion.60
  390.2 8.3 fusion.48
  398.9 5.4 fusion.59
  406.3 20.8 %all-gather.12.cloned.1.call-done = bf16[2048,512]{1,0:T(8,128)(2,1)} async-done(((bf16[512,512]{1,0:T(8,128)(2,1)}), bf16[2048,512]{1,0:T(8,128)(2,1)}) %all-gather.12.cloned.1.call-update) | async-done | bytes 2097168 | tf_op jit(solution)/shard_map/all_gather | solution.py:218
  427.2 7.5 convert_reduce_fusion
  439.4 44.6 %reduce-scatter.10.cloned.1.call-done = f32[512,512]{1,0:T(8,128)} async-done(((f32[2048,512]{1,0:T(8,128)}), f32[512,512]{1,0:T(8,128)}) %reduce-scatter.10.cloned.1.call-update) | async-done | bytes 1048592 | tf_op jit(solution)/shard_map/reduce_scatter | solution.py:228
  489.0 22.6 %all-gather.14.cloned.1.call-done = bf16[2048,512]{1,0:T(8,128)(2,1)} async-done(((bf16[512,512]{1,0:T(8,128)(2,1)}), bf16[2048,512]{1,0:T(8,128)(2,1)}) %all-gather.14.cloned.1.call-update) | async-done | bytes 2097168 | tf_op jit(solution)/shard_map/all_gather | solution.py:238
  514.0 231.9 %while.35 = (s32[]{:T(128)}, f32[4,512,128]{1,2,0:T(8,128)}, f32[4,512,128]{1,2,0:T(8,128)}, bf16[4,1024,128]{1,2,0:T(8,128)(2,1)}, bf16[4,1024,128]{1,2,0:T(8,1...) while((s32[]{:T(128)}, f32[4,512,128]{1,2,0:T(8,128)}, ...), condition=%wide.region_21.22_spmd, body=%wide.region_19.21_spmd.sunk | while | flops 1086326272 | bytes 130603432 | solution.py:307
  530.2 7.9 reshape.544
  538.1 4.7 slice.42
  542.8 5.3 reshape.545
  560.1 5.8 reshape.547
  588.0 7.9 reshape.544
  600.6 5.3 reshape.545
  617.9 5.8 reshape.547
  645.9 7.9 reshape.544
  658.4 5.3 reshape.545
  675.7 5.8 reshape.547
  703.7 7.9 reshape.544
  716.3 5.3 reshape.545
  733.6 5.8 reshape.547
  760.5 5.0 fusion.99
  782.2 22.1 %all-reduce.4 = (f32[128]{0:T(128)}, f32[128]{0:T(128)}, f32[512]{0:T(512)}) all-reduce(f32[128]{0:T(128)S(1)} %get-tuple-element.541, f32[128]{0:T(128)S(1)} %get-tuple-element.539, f32[512]{0:T(512)S(1)} %copy-done.93), channel_id=1, replica_groups=mesh['dp'=8,'mp'=4] {'dp'}, use_global_device_ids=true, to_apply=%region_38.39 | all-reduce | flops 768 | bytes 6144 | tf_op jit(solution)/shard_map/psum | solution.py:367
  805.8 16.1 %reduce-scatter.14.cloned.1.call-done = bf16[4,128,512]{2,1,0:T(8,128)(2,1)} async-done(((bf16[4,512,512]{2,1,0:T(8,128)(2,1)}), bf16[4,128,512]{2,1,0:T(8,128)(2,1)}) %reduce-scatter.14.cloned.1.call-update) | async-done | bytes 524304 | tf_op jit(solution)/shard_map/reduce_scatter | solution.py:353
  824.1 43.8 %all-reduce.3 = (f32[512]{0:T(512)}, f32[512]{0:T(512)}, f32[512]{0:T(512)}, f32[512]{0:T(512)}, f32[512]{0:T(512)}, /*index=5*/f32[512]{0:T(512)}) all-reduce(f32[512]{0:T(512)S(1)} %add.318, f32[512]{0:T(512)S(1)} %add.319, f32[512]{0:T(512)S(1)} %copy-done.90, f32[512]{0:T(512)S(1)} %copy-done.91, ...), channel_id=1, replica_groups=mesh['dp'=8,'mp'=4] {'dp','mp'}, use_global_device_ids=true, to_apply=%region_28.29 | all-reduce | flops 3072 | bytes 24576 | tf_op jit(solution)/shard_map/psum | solution.py:382
  870.5 97.8 %all-reduce.8.cloned.1.call-done = (f32[512,128]{1,0:T(8,128)}, f32[512,128]{1,0:T(8,128)}, f32[512,128]{1,0:T(8,128)}, f32[512,128]{1,0:T(8,128)}, f32[128,512]...) async-done(((f32[512,128]{1,0:T(8,128)}, f32[512,128]{1,0:T(8,128)}, f32[512,128]{1,0:T(8,128)}, f32[512,128]{1,0:T(8,128)}, f32[128,512]{1,0:T(8,128)}, ...) | async-done | bytes 3407888 | tf_op jit(solution)/shard_map/psum | solution.py:367
  (552 shorter events, 332.4 us)
Async XLA Ops:
  7.2 282.1 %copy-start = (bf16[512,512]{1,0:T(8,128)(2,1)S(1)}, bf16[512,512]{1,0:T(8,128)(2,1)}, u32[]{:S(2)}) copy-start(bf16[512,512]{1,0:T(8,128)(2,1)} %param.49) | copy-start | bytes 1572868
  7.2 31.4 %all-gather.8.cloned.1.call-start = ((), (), s32[]{:S(2)}) async-start(), calls=%async_computation.8 | async-start | bytes 2621440 | tf_op jit(solution)/shard_map/all_gather | solution.py:140
  13.2 50.2 %all-gather.6.cloned.1.call-start = ((), (), s32[]{:S(2)}) async-start(), calls=%async_computation.7 | async-start | bytes 2621440 | tf_op jit(solution)/shard_map/all_gather | solution.py:141
  15.6 47.8 %copy-start.43 = (bf16[512,128]{1,0:T(8,128)(2,1)S(1)}, bf16[512,128]{1,0:T(8,128)(2,1)}, u32[]{:S(2)}) copy-start(bf16[512,128]{1,0:T(8,128)(2,1)} %param.41) | copy-start | bytes 393220
  15.6 246.7 %reduce-scatter.6.cloned.1.call-start = ((), (), s32[]{:S(2)}) async-start(), calls=%async_computation.9 | async-start | bytes 5242880 | tf_op jit(solution)/shard_map/reduce_scatter | solution.py:184
  76.7 136.8 %copy-start.42 = (bf16[128,512]{1,0:T(8,128)(2,1)S(1)}, bf16[128,512]{1,0:T(8,128)(2,1)}, u32[]{:S(2)}) copy-start(bf16[128,512]{1,0:T(8,128)(2,1)} %param.46) | copy-start | bytes 393220
  217.6 44.7 %copy-start.7 = (bf16[512,512]{1,0:T(8,128)(2,1)S(1)}, bf16[512,512]{1,0:T(8,128)(2,1)}, u32[]{:S(2)}) copy-start(bf16[512,512]{1,0:T(8,128)(2,1)} %param.29) | copy-start | bytes 1572868
  217.6 47.0 %copy-start.82 = (f32[512]{0:T(512)S(1)}, f32[512]{0:T(512)}, u32[]{:S(2)}) copy-start(f32[512]{0:T(512)} %param.47) | copy-start | bytes 6148
  217.6 47.0 %copy-start.92 = (f32[512]{0:T(512)S(1)}, f32[512]{0:T(512)}, u32[]{:S(2)}) copy-start(f32[512]{0:T(512)} %param.48) | copy-start | bytes 6148
  217.7 48.1 %copy-start.85 = (s32[8,256]{1,0:T(8,128)S(1)}, s32[8,256]{1,0:T(8,128)}, u32[]{:S(2)}) copy-start(s32[8,256]{1,0:T(8,128)} %param.33) | copy-start | bytes 24580
  217.7 54.2 %copy-start.96 = (bf16[512]{0:T(512)(128)(2,1)S(1)}, bf16[512]{0:T(512)(128)(2,1)}, u32[]{:S(2)}) copy-start(bf16[512]{0:T(512)(128)(2,1)} %param.50) | copy-start | bytes 3076
  217.7 71.6 %all-gather.10.cloned.1.call-start = ((), (), s32[]{:S(2)}) async-start(), calls=%async_computation.10 | async-start | bytes 2621440 | tf_op jit(solution)/shard_map/all_gather | solution.py:191
  263.7 25.6 %copy-start.55 = (f32[512]{0:T(512)}, f32[512]{0:T(512)S(1)}, u32[]{:S(2)}) copy-start(f32[512]{0:T(512)S(1)} %broadcast_multiply_fusion) | copy-start | bytes 6148
  266.3 12.0 %all-to-all-start = ((s32[8,1,256]{2,1,0:T(1,128)}), s32[8,1,256]{2,1,0:T(1,128)S(1)}, u32[]{:S(2)}, u32[]{:S(2)}) async-start(s32[8,1,256]{2,1,0:T(1,128)} %all_to_all.13), calls=%async_computation.2 | async-start | bytes 16384 | tf_op jit(solution)/shard_map/all_to_all | solution.py:125
  271.9 97.5 %reduce-scatter.8.cloned.1.call-start = ((), (), s32[]{:S(2)}) async-start(), calls=%async_computation.11 | async-start | bytes 2621440 | tf_op jit(solution)/shard_map/reduce_scatter | solution.py:196
  271.9 17.4 %copy-start.94 = (f32[512]{0:T(512)}, f32[512]{0:T(512)S(1)}, u32[]{:S(2)}) copy-start(f32[512]{0:T(512)S(1)} %convert_element_type.164) | copy-start | bytes 6148
  300.7 53.5 %all-to-all-start.1 = ((bf16[8,256,512]{2,1,0:T(8,128)(2,1)}), bf16[8,256,512]{2,1,0:T(8,128)(2,1)}, u32[]{:S(2)}, u32[]{:S(2)}) async-start(bf16[8,256,512]{2,1,0:T(8,128)(2,1)} %broadcast_select_fusion), calls=%async_computation.3 | async-start | bytes 4194304 | tf_op jit(solution)/shard_map/all_to_all | solution.py:128
  305.5 121.7 %all-gather.12.cloned.1.call-start = ((), (), s32[]{:S(2)}) async-start(), calls=%async_computation.12 | async-start | bytes 2621440 | tf_op jit(solution)/shard_map/all_gather | solution.py:218
  306.3 64.4 %copy-start.48 = (pred[512,4]{1,0:T(8,128)(4,1)}, pred[512,4]{1,0:T(8,128)(4,1)S(1)}, u32[]{:S(2)}) copy-start(pred[512,4]{1,0:T(8,128)(4,1)S(1)} %copy.116) | copy-start | bytes 6148
  370.7 17.5 %copy-start.12 = (f32[512,512]{1,0:T(8,128)}, f32[512,512]{1,0:T(8,128)S(1)}, u32[]{:S(2)}) copy-start(f32[512,512]{1,0:T(8,128)S(1)} %add_add_fusion.4) | copy-start | bytes 3145732
  371.1 9.1 copy-start.87
  379.5 8.7 copy-start.53
  405.3 81.6 %copy-start.10 = (f32[512,512]{1,0:T(8,128)}, f32[512,512]{1,0:T(8,128)S(1)}, u32[]{:S(2)}) copy-start(f32[512,512]{1,0:T(8,128)S(1)} %get-tuple-element.518) | copy-start | bytes 3145732
  406.3 77.8 %reduce-scatter.10.cloned.1.call-start = ((), (), s32[]{:S(2)}) async-start(), calls=%async_computation.13 | async-start | bytes 5242880 | tf_op jit(solution)/shard_map/reduce_scatter | solution.py:228
  439.4 44.7 %copy-start.56 = (f32[512]{0:T(512)S(1)}, f32[512]{0:T(512)}, u32[]{:S(2)}) copy-start(f32[512]{0:T(512)} %copy-done.55) | copy-start | bytes 6148
  439.4 44.7 %copy-start.65 = (f32[512]{0:T(512)S(1)}, f32[512]{0:T(512)}, u32[]{:S(2)}) copy-start(f32[512]{0:T(512)} %copy-done.64) | copy-start | bytes 6148
  439.4 44.7 %copy-start.83 = (f32[512]{0:T(512)S(1)}, f32[512]{0:T(512)}, u32[]{:S(2)}) copy-start(f32[512]{0:T(512)} %param.47) | copy-start | bytes 6148
  439.4 47.0 %copy-start.73 = (f32[512]{0:T(512)S(1)}, f32[512]{0:T(512)}, u32[]{:S(2)}) copy-start(f32[512]{0:T(512)} %copy-done.72) | copy-start | bytes 6148
  439.4 72.3 %all-gather.14.cloned.1.call-start = ((), (), s32[]{:S(2)}) async-start(), calls=%async_computation.14 | async-start | bytes 2621440 | tf_op jit(solution)/shard_map/all_gather | solution.py:238
  486.9 27.1 %copy-start.66 = (f32[512]{0:T(512)}, f32[512]{0:T(512)S(1)}, u32[]{:S(2)}) copy-start(f32[512]{0:T(512)S(1)} %negate_multiply_fusion.1) | copy-start | bytes 6148
  488.9 315.4 %reduce-scatter.12.cloned.1.call-start = ((), (), s32[]{:S(2)}) async-start(), calls=%async_computation.15 | async-start | bytes 2621440 | tf_op jit(solution)/shard_map/reduce_scatter | solution.py:347
  756.5 65.4 %reduce-scatter.14.cloned.1.call-start = ((), (), s32[]{:S(2)}) async-start(), calls=%async_computation.16 | async-start | bytes 2621440 | tf_op jit(solution)/shard_map/reduce_scatter | solution.py:353
  760.5 207.9 %all-reduce.8.cloned.1.call-start = ((), (), s32[]{:S(2)}) async-start(), calls=%async_computation.17 | async-start | bytes 6815744 | tf_op jit(solution)/shard_map/psum | solution.py:367
  780.4 23.9 %copy-start.8 = (bf16[512,512]{1,0:T(8,128)(2,1)S(1)}, bf16[512,512]{1,0:T(8,128)(2,1)}, u32[]{:S(2)}) copy-start(bf16[512,512]{1,0:T(8,128)(2,1)} %param.29) | copy-start | bytes 1572868
  780.4 23.9 %copy-start.47 = (f32[512]{0:T(512)S(1)}, f32[512]{0:T(512)}, u32[]{:S(2)}) copy-start(f32[512]{0:T(512)} %copy-done.46) | copy-start | bytes 6148
  780.4 23.9 %copy-start.52 = (f32[512]{0:T(512)S(1)}, f32[512]{0:T(512)}, u32[]{:S(2)}) copy-start(f32[512]{0:T(512)} %param.38) | copy-start | bytes 6148
  780.4 41.5 %copy-start.19 = (bf16[4,128,512]{2,1,0:T(8,128)(2,1)S(1)}, bf16[4,128,512]{2,1,0:T(8,128)(2,1)}, u32[]{:S(2)}) copy-start(bf16[4,128,512]{2,1,0:T(8,128)(2,1)} %param.30) | copy-start | bytes 1572868
  780.5 41.5 %copy-start.60 = (f32[4,128]{1,0:T(4,128)S(1)}, f32[4,128]{1,0:T(4,128)}, u32[]{:S(2)}) copy-start(f32[4,128]{1,0:T(4,128)} %copy-done.59) | copy-start | bytes 6148
  780.5 41.5 %copy-start.69 = (f32[4,128]{1,0:T(4,128)S(1)}, f32[4,128]{1,0:T(4,128)}, u32[]{:S(2)}) copy-start(f32[4,128]{1,0:T(4,128)} %copy-done.68) | copy-start | bytes 6148
  780.5 42.8 %copy-start.71 = (f32[512]{0:T(512)S(1)}, f32[512]{0:T(512)}, u32[]{:S(2)}) copy-start(f32[512]{0:T(512)} %copy-done.70) | copy-start | bytes 6148
  780.5 42.8 %copy-start.58 = (f32[512]{0:T(512)S(1)}, f32[512]{0:T(512)}, u32[]{:S(2)}) copy-start(f32[512]{0:T(512)} %copy-done.57) | copy-start | bytes 6148
  780.5 43.5 %copy-start.89 = (f32[512]{0:T(512)S(1)}, f32[512]{0:T(512)}, u32[]{:S(2)}) copy-start(f32[512]{0:T(512)} %get-tuple-element.517) | copy-start | bytes 6148
  780.5 43.5 %copy-start.90 = (f32[512]{0:T(512)S(1)}, f32[512]{0:T(512)}, u32[]{:S(2)}) copy-start(f32[512]{0:T(512)} %get-tuple-element.440) | copy-start | bytes 6148
  780.5 43.5 %copy-start.91 = (f32[512]{0:T(512)S(1)}, f32[512]{0:T(512)}, u32[]{:S(2)}) copy-start(f32[512]{0:T(512)} %get-tuple-element.444) | copy-start | bytes 6148
  780.6 87.3 %copy-start.11 = (f32[512,512]{1,0:T(8,128)S(1)}, f32[512,512]{1,0:T(8,128)}, u32[]{:S(2)}) copy-start(f32[512,512]{1,0:T(8,128)} %copy-done.10) | copy-start | bytes 3145732
  780.6 87.3 %copy-start.67 = (f32[512]{0:T(512)S(1)}, f32[512]{0:T(512)}, u32[]{:S(2)}) copy-start(f32[512]{0:T(512)} %copy-done.66) | copy-start | bytes 6148
  804.3 19.0 %copy-start.22 = (bf16[512,512]{1,0:T(8,128)(2,1)S(1)}, bf16[512,512]{1,0:T(8,128)(2,1)}, u32[]{:S(2)}) copy-start(bf16[512,512]{1,0:T(8,128)(2,1)} %reduce-scatter.12.cloned.1.call-done) | copy-start | bytes 1572868
  968.3 9.5 copy-start.35
  (87 other events, 359.1 us)
Sparse Core Ops, SparseCore 0:
  13.3 25.2 all-gather.7
  40.8 22.5 all-gather.5
  217.7 44.4 reduce-scatter.5
  265.8 22.5 all-gather.9
  299.3 30.5 reduce-scatter.7
  406.4 20.7 all-gather.11
  439.5 44.4 reduce-scatter.9
  489.0 22.5 all-gather.13
  756.6 31.4 reduce-scatter.11
  790.5 31.4 reduce-scatter.13
  828.4 139.8 all-reduce.7
where the time goes:
time: 994 us; the launch traced here: 986 us
  waiting for transfers between devices  341 us (34%)
  local copies, waits for them, and re-layouts  324 us (33%)
  matrix products  166 us (17%)
  blocking collectives  65.9 us (7%)
  other arithmetic  49.7 us (5%)
  between operations  15.3 us (2%)
  loops' own time  12.1 us (1%)
  starting transfers between devices  10.7 us (1%)
    psum x1, waiting for transfers between devices, local(): lax.psum((grad_query_weight, grad_key_weight, grad_value_weight, grad_pos...  97.8 us
    reshape x12, local copies, waits for them, and re-layouts, shift_rows(): folded = padded.reshape(leading + (KEYS + 1, SEG))[..., 1:, :]  85.9 us
    reshape x12, local copies, waits for them, and re-layouts, shift_rows(): return folded.reshape(leading + (SEG, KEYS))  51.6 us
    all_to_all x1, waiting for transfers between devices, local(): lax.all_to_all(found, 'dp', split_axis=0, concat_axis=0, tiled=True)  46.2 us
    reduce_scatter x1, waiting for transfers between devices, local(): lax.psum_scatter(jnp.einsum('tf,df->td', grad_preact, inner_weight, prefe...  44.6 us
    reduce_scatter x1, waiting for transfers between devices, local(): lax.psum_scatter(jnp.dot(attended_low, out_proj, preferred_element_type=j...  44.6 us
    psum x1, blocking collectives, local(): lax.psum((gain_from_input + gain_from_memory, bias_from_input + bias_from...  43.8 us
    dynamic_slice x48, local copies, waits for them, and re-layouts, local(): lax.map(attend, (content_q, position_q, key_rows, value_rows, memory_leng...  38.2 us
  transfers between devices with their start and end apart: 13, of which 10 were waited for; matrix products, arithmetic and copies ran while one was open for 7% of the time, Pallas kernels for 0%

commit v1 on v0

v1 whole, which is shorter than its diff:
```python
import math

import jax
import jax.numpy as jnp
import numpy as np
from jax import lax
from jax.experimental import pallas as pl
from jax.experimental.pallas import tpu as pltpu
from jax.sharding import PartitionSpec as P

D = 512
HD = 64
SEG = 512
MEM = 512
KEYS = 1024
SLOT = 128
EPS = 1e-05
F32 = jnp.float32
BF16 = jnp.bfloat16
GELU_C = math.sqrt(2.0 / math.pi)
SCALE = HD ** (-0.5)
VMEM = pl.BlockSpec(memory_space=pltpu.VMEM)
SMEM = pl.BlockSpec(memory_space=pltpu.SMEM)


def position_table():
    distance = (KEYS - 1 - np.arange(KEYS)).astype(np.float32)
    exponent = np.arange(0, D, 2).astype(np.float32) / np.float32(D)
    angles = distance[:, None] * np.exp(np.float32(-math.log(10000.0)) * exponent)[None, :]
    table = np.concatenate([np.sin(angles), np.cos(angles)], axis=1).astype(np.float32)
    return jnp.asarray(table).astype(BF16)


def call(body, outs, ins, flops=0, scratch=(), smem=0, vmem=56):
    nbytes = sum(a.size * a.dtype.itemsize for a in ins)
    return pl.pallas_call(
        body,
        out_shape=outs,
        in_specs=[SMEM] * smem + [VMEM] * (len(ins) - smem),
        out_specs=jax.tree.map(lambda _: VMEM, outs),
        scratch_shapes=list(scratch),
        compiler_params=pltpu.CompilerParams(vmem_limit_bytes=vmem * 2**20),
        cost_estimate=pl.CostEstimate(flops=flops, bytes_accessed=nbytes, transcendentals=0),
    )(*ins)


def shape(dims, dtype):
    return jax.ShapeDtypeStruct(dims, dtype)


def mm(a, b):
    return jnp.dot(a, b, preferred_element_type=F32)


def mm_nt(a, b):
    return lax.dot_general(a, b, (((1,), (1,)), ((), ())), preferred_element_type=F32)


def mm_tn(a, b):
    return lax.dot_general(a, b, (((0,), (0,)), ((), ())), preferred_element_type=F32)


def mm_tt(a, b):
    return lax.dot_general(a, b, (((0,), (1,)), ((), ())), preferred_element_type=F32)


def norm_parts(values):
    average = jnp.mean(values, axis=-1, keepdims=True)
    centred = values - average
    spread = jnp.mean(centred * centred, axis=-1, keepdims=True)
    inverse = lax.rsqrt(spread + EPS)
    return centred * inverse, inverse


def norm_back(grad, gain, xhat, inverse):
    scaled = grad * gain
    return inverse * (
        scaled
        - jnp.mean(scaled, axis=-1, keepdims=True)
        - xhat * jnp.mean(scaled * xhat, axis=-1, keepdims=True)
    )


def head_lanes(rows, h):
    lane = lax.broadcasted_iota(jnp.int32, (rows, SLOT), 1)
    return (lane // HD) == h


def of_head(values, h):
    return jnp.where(head_lanes(values.shape[0], h), values, jnp.zeros_like(values))


def norm_kernel(place_ref, x_ref, m0, m1, m2, m3, g_ref, b_ref, keys_ref):
    me = place_ref[0]
    gain, bias = g_ref[...], b_ref[...]
    for k, block in enumerate((m0, m1, m2, m3)):
        xhat, _ = norm_parts(block[...].astype(F32))
        start = pl.multiple_of((me ^ k) * SLOT, SLOT)
        keys_ref[pl.ds(start, SLOT), :] = (xhat * gain + bias).astype(BF16)
    xhat, _ = norm_parts(x_ref[...].astype(F32))
    keys_ref[MEM:, :] = (xhat * gain + bias).astype(BF16)


def attend_kernel(
    place_ref, mem_ref, doc_ref,
    keys_ref, table_ref, q0, q1, k0, k1, v0, v1, p0, p1, s0, s1,
    probs_ref, qc_ref, qp_ref, kr_ref, vr_ref, pk_ref, att_ref,
    bias_ref,
):
    row = place_ref[0]
    low = MEM - mem_ref[row]
    high = MEM + doc_ref[row]
    place_k = lax.broadcasted_iota(jnp.int32, (SEG, KEYS), 1)
    place_q = lax.broadcasted_iota(jnp.int32, (SEG, KEYS), 0)
    live = (place_k >= low) & (place_k <= MEM + place_q) & (place_k < high)
    bias_ref[...] = jnp.where(live, 0.0, -1e30)
    keys_in = keys_ref[...]
    normed = keys_ref[MEM:, :]
    for s, (wq, wk, wv, wp, small) in enumerate(
        ((q0, k0, v0, p0, s0), (q1, k1, v1, p1, s1))
    ):
        query = mm(normed, wq[...])
        qc_ref[s] = (query + small[1:2, :SLOT]).astype(BF16)
        qp_ref[s] = (query + small[1:2, SLOT : 2 * SLOT]).astype(BF16)
        kr_ref[s] = mm(keys_in, wk[...]).astype(BF16)
        vr_ref[s] = mm(keys_in, wv[...]).astype(BF16)
        pk_ref[s] = mm(table_ref[...], wp[...]).astype(BF16)
    for s in range(2):
        parts = []
        for h in range(2):
            content = mm_nt(of_head(qc_ref[s], h), kr_ref[s])
            place = mm_nt(of_head(qp_ref[s], h), pk_ref[s])
            place = pltpu.roll(place, KEYS - SEG + 1, 1, stride=1, stride_axis=0)
            scores = (content + place) * SCALE + bias_ref[...]
            largest = jnp.max(scores, axis=-1, keepdims=True)
            raised = jnp.exp(scores - largest)
            total = jnp.sum(raised, axis=-1, keepdims=True)
            probs = (raised * (1.0 / total)).astype(BF16)
            probs_ref[2 * s + h] = probs
            parts.append(mm(probs, vr_ref[s]))
        att_ref[s] = jnp.where(head_lanes(SEG, 0), parts[0], parts[1]).astype(BF16)


def feed_kernel(
    x_ref, att_a, att_b, o0, o1, o2, o3, g_ref, b_ref,
    i0, i1, i2, i3, s0, s1, s2, s3, u0, u1, u2, u3, ob_ref,
    middle_ref, hidden_ref, nm_ref, act_ref, slope_ref,
):
    middle = x_ref[...].astype(F32)
    for att, w in ((att_a[0], o0), (att_a[1], o1), (att_b[0], o2), (att_b[1], o3)):
        middle = middle + mm(att, w[...])
    middle_ref[...] = middle
    xhat, _ = norm_parts(middle)
    normed = (xhat * g_ref[...] + b_ref[...]).astype(BF16)
    nm_ref[...] = normed
    hidden = middle + ob_ref[...]
    for s, (wi, small, wo) in enumerate(((i0, s0, u0), (i1, s1, u1), (i2, s2, u2), (i3, s3, u3))):
        pre = mm(normed, wi[...]) + small[0:1, :]
        square = pre * pre
        bend = jnp.tanh(GELU_C * (pre + 0.044715 * (pre * square)))
        act = (0.5 * pre * (1.0 + bend)).astype(BF16)
        slope = 0.5 * (1.0 + bend) + (0.5 * GELU_C) * pre * (1.0 - bend * bend) * (
            1.0 + (3 * 0.044715) * square
        )
        act_ref[s] = act
        slope_ref[s] = slope.astype(BF16)
        hidden = hidden + mm(act, wo[...])
    hidden_ref[...] = hidden


def mix_kernel(blocks, *refs):
    place_ref, doc_ref = refs[:2]
    fetched_refs = refs[2 : 2 + blocks]
    (
        slots_ref, cot_ref, hidden_ref, gate_ref,
        mixed_ref, gh_ref, gate_grad_ref, fetched,
    ) = refs[2 + blocks :]
    rows = fetched_refs[0].shape[0]
    for n, block in enumerate(fetched_refs):
        fetched[n * rows : (n + 1) * rows, :] = block[...]
    total = blocks * rows
    docs = doc_ref[place_ref[0]]
    gate = gate_ref[...]
    scale = 1.0 / math.sqrt(D)
    step = 128
    gate_grad = jnp.zeros((1, D), F32)
    for c in range(SEG // step):
        span = slice(c * step, (c + 1) * step)
        lane = lax.broadcasted_iota(jnp.int32, (step, total), 1)
        near = []
        for j in range(4):
            pick = jnp.where(slots_ref[span, j : j + 1] == lane, 1.0, 0.0).astype(BF16)
            near.append(mm(pick, fetched[...]))
        hidden = hidden_ref[span, :]
        token = c * step + lax.broadcasted_iota(jnp.int32, (step, 1), 0)
        grad_mixed = cot_ref[span, :].astype(F32) * jnp.where(token < docs, 1.0, 0.0)
        rel = [jnp.sum(hidden * n, axis=-1, keepdims=True) * scale for n in near]
        top = jnp.maximum(jnp.maximum(rel[0], rel[1]), jnp.maximum(rel[2], rel[3]))
        raised = [jnp.exp(r - top) for r in rel]
        inverse = 1.0 / (raised[0] + raised[1] + raised[2] + raised[3])
        alpha = [r * inverse for r in raised]
        recalled = sum(a * n for a, n in zip(alpha, near))
        logit = jnp.sum(hidden * gate, axis=-1, keepdims=True)
        gating = 1.0 / (1.0 + jnp.exp(-logit))
        apart = recalled - hidden
        mixed_ref[span, :] = (hidden + gating * apart).astype(BF16)
        grad_recalled = gating * grad_mixed
        grad_gating = jnp.sum(grad_mixed * apart, axis=-1, keepdims=True)
        grad_logit = grad_gating * gating * (1.0 - gating)
        grad_alpha = [jnp.sum(grad_recalled * n, axis=-1, keepdims=True) for n in near]
        weighed = sum(a * g for a, g in zip(alpha, grad_alpha))
        grad_rel = [a * (g - weighed) * scale for a, g in zip(alpha, grad_alpha)]
        grad_hidden = grad_mixed - grad_recalled + grad_logit * gate
        grad_hidden = grad_hidden + sum(g * n for g, n in zip(grad_rel, near))
        gh_ref[span, :] = grad_hidden
        gate_grad = gate_grad + jnp.sum(grad_logit * hidden, axis=0, keepdims=True)
    gate_grad_ref[...] = gate_grad


FEED_ROWS = 2 * D + SLOT + 64


def feed_back_kernel(
    gh_ref, gate_grad_ref, middle_ref, nm_ref, act_ref, slope_ref, g_ref,
    att_a, att_b, o0, o1, o2, o3, i0, i1, i2, i3, u0, u1, u2, u3,
    gm_ref, ga_a, ga_b, pay_ref,
):
    grad_hidden = gh_ref[...]
    low = grad_hidden.astype(BF16)
    low_t = low.T
    normed_t = nm_ref[...].T
    outer_bias_grad = jnp.sum(grad_hidden, axis=0, keepdims=True)
    grad_nm = jnp.zeros((SEG, D), F32)
    bias_rows = []
    for s, (wi, wo) in enumerate(((i0, u0), (i1, u1), (i2, u2), (i3, u3))):
        grad_act = mm_nt(low, wo[...])
        grad_pre = (grad_act * slope_ref[s].astype(F32)).astype(BF16)
        pay_ref[s, D : 2 * D, :] = mm(low_t, act_ref[s]).astype(BF16)
        pay_ref[s, 0:D, :] = mm(normed_t, grad_pre).astype(BF16)
        bias_rows.append(jnp.sum(grad_pre.astype(F32), axis=0, keepdims=True))
        grad_nm = grad_nm + mm_nt(grad_pre, wi[...])
    xhat, inverse = norm_parts(middle_ref[...])
    gain_grad = jnp.sum(grad_nm * xhat, axis=0, keepdims=True)
    bias_grad = jnp.sum(grad_nm, axis=0, keepdims=True)
    grad_middle = grad_hidden + norm_back(grad_nm, g_ref[...], xhat, inverse)
    gm_ref[...] = grad_middle
    middle_low = grad_middle.astype(BF16)
    zeros = jnp.zeros((59, D), F32)
    for s, (att, w) in enumerate(
        ((att_a[0], o0), (att_a[1], o1), (att_b[0], o2), (att_b[1], o3))
    ):
        pay_ref[s, 2 * D : 2 * D + SLOT, :] = mm_tn(att, middle_low).astype(BF16)
        grad_att = mm_nt(middle_low, w[...]).astype(BF16)
        (ga_a if s < 2 else ga_b)[s % 2] = grad_att
        tail = jnp.concatenate(
            [bias_rows[s], gain_grad, bias_grad, outer_bias_grad, gate_grad_ref[...], zeros], axis=0
        )
        pay_ref[s, 2 * D + SLOT :, :] = tail.astype(BF16)


HEAD_ROWS = 4 * SLOT + 64


def attend_back_kernel(
    last,
    *refs,
):
    (
        keys_ref, table_ref, probs_ref, qc_ref, qp_ref, kr_ref, vr_ref, pk_ref, ga_ref,
        q0, q1, k0, k1, v0, v1,
    ) = refs[:15]
    if last:
        dk_in, gm_ref, x_ref, m0, m1, m2, m3, place_ref, g_ref = refs[15:24]
        pay_ref, grad_ref = refs[24:26]
        dk_ref = refs[26]
    else:
        pay_ref, dk_ref = refs[15:17]
    half = SEG // 2
    across = lax.broadcasted_iota(jnp.int32, (half, half), 1)
    down = lax.broadcasted_iota(jnp.int32, (half, half), 0)
    swap = jnp.where(across + down == half - 1, 1.0, 0.0).astype(BF16)

    def flip(values):
        return jnp.concatenate([mm(swap, values[half:]), mm(swap, values[:half])], axis=0)

    keys_in = keys_ref[...]
    normed = keys_ref[MEM:, :]
    for s, (wq, wk, wv) in enumerate(((q0, k0, v0), (q1, k1, v1))):
        grad_v = jnp.zeros((SLOT, KEYS), F32)
        grad_k = jnp.zeros((SLOT, KEYS), F32)
        grad_p = jnp.zeros((SLOT, KEYS), F32)
        grad_c = jnp.zeros((SEG, SLOT), F32)
        grad_place = jnp.zeros((SEG, SLOT), F32)
        qp_flip = flip(qp_ref[s]).astype(BF16)
        for h in range(2):
            probs = probs_ref[2 * s + h]
            grad_out = of_head(ga_ref[s], h)
            grad_probs = mm_nt(grad_out, vr_ref[s])
            wide = probs.astype(F32)
            weighed = jnp.sum(wide * grad_probs, axis=-1, keepdims=True)
            grad_scores = (wide * (grad_probs - weighed)).astype(BF16)
            grad_v = grad_v + mm_tn(grad_out, probs)
            grad_k = grad_k + mm_tn(of_head(qc_ref[s], h), grad_scores)
            grad_c = grad_c + mm(grad_scores, of_head(kr_ref[s], h))
            turned = pltpu.roll(flip(grad_scores), 0, 1, stride=1, stride_axis=0).astype(BF16)
            grad_place = grad_place + mm(turned, of_head(pk_ref[s], h))
            grad_p = grad_p + mm_tn(of_head(qp_flip, h), turned)
        grad_v = grad_v.astype(BF16)
        grad_k = (grad_k * SCALE).astype(BF16)
        grad_p = (grad_p * SCALE).astype(BF16)
        grad_c = grad_c * SCALE
        grad_place = grad_place * SCALE
        high = grad_place.astype(BF16)
        rest = (grad_place - high.astype(F32)).astype(BF16)
        grad_q = (grad_c + flip(high) + flip(rest)).astype(BF16)
        pay_ref[s, 0:SLOT, :] = mm_tn(grad_q, normed).astype(BF16)
        pay_ref[s, SLOT : 2 * SLOT, :] = mm(grad_k, keys_in).astype(BF16)
        pay_ref[s, 2 * SLOT : 3 * SLOT, :] = mm(grad_v, keys_in).astype(BF16)
        pay_ref[s, 3 * SLOT : 4 * SLOT, :] = mm(grad_p, table_ref[...]).astype(BF16)
        biases = jnp.concatenate(
            [
                jnp.sum(grad_c, axis=0, keepdims=True),
                jnp.sum(grad_place, axis=0, keepdims=True),
                jnp.zeros((1, D - 2 * SLOT), F32),
            ],
            axis=1,
        )
        pay_ref[s, 4 * SLOT :, :] = jnp.concatenate(
            [biases, jnp.zeros((63, D), F32)], axis=0
        ).astype(BF16)
        both = jnp.concatenate([grad_k, grad_v], axis=0)
        weights = jnp.concatenate([wk[...], wv[...]], axis=1)
        grad_keys = mm_tt(both, weights)
        grad_rows = mm_nt(grad_q, wq[...])
        if s == 0 and not last:
            dk_ref[:MEM, :] = grad_keys[:MEM]
            dk_ref[MEM:, :] = grad_keys[MEM:] + grad_rows
        else:
            before = dk_in if (s == 0) else dk_ref
            dk_ref[:MEM, :] = before[:MEM, :] + grad_keys[:MEM]
            dk_ref[MEM:, :] = before[MEM:, :] + grad_keys[MEM:] + grad_rows
    if last:
        gain = g_ref[...]
        me = place_ref[0]
        xhat, inverse = norm_parts(x_ref[...].astype(F32))
        grad = dk_ref[MEM:, :]
        grad_ref[...] = gm_ref[...] + norm_back(grad, gain, xhat, inverse)
        gain_grad = jnp.sum(grad * xhat, axis=0, keepdims=True)
        bias_grad = jnp.sum(dk_ref[...], axis=0, keepdims=True)
        for k, block in enumerate((m0, m1, m2, m3)):
            xhat, _ = norm_parts(block[...].astype(F32))
            start = pl.multiple_of((me ^ k) * SLOT, SLOT)
            gain_grad = gain_grad + jnp.sum(
                dk_ref[pl.ds(start, SLOT), :] * xhat, axis=0, keepdims=True
            )
        tail = jnp.concatenate([gain_grad, bias_grad], axis=0)
        for s in range(2):
            pay_ref[s, 4 * SLOT + 8 : 4 * SLOT + 16, :] = jnp.concatenate(
                [tail, jnp.zeros((6, D), F32)], axis=0
            ).astype(BF16)


def swap_with(values, axis, k):
    n = lax.axis_size(axis)
    return lax.ppermute(values, axis, [(i, i ^ k) for i in range(n)])


def add_low(*terms):
    return sum(t.astype(F32) for t in terms).astype(BF16)


def sum_over(values, axis):
    n = lax.axis_size(axis)
    me = lax.axis_index(axis)
    steps = []
    k = 1
    while k < min(n, 8) and values.shape[0] % 16 == 0:
        half = values.shape[0] // 2
        bit = (me // k) % 2
        sent = lax.dynamic_slice_in_dim(values, (1 - bit) * half, half)
        kept = lax.dynamic_slice_in_dim(values, bit * half, half)
        values = add_low(kept, swap_with(sent, axis, k))
        steps.append((k, bit))
        k *= 2
    while k < n:
        values = add_low(values, swap_with(values, axis, k))
        k *= 2
    for k, bit in reversed(steps):
        other = swap_with(values, axis, k)
        first = jnp.where(bit == 0, values, other)
        second = jnp.where(bit == 0, other, values)
        values = jnp.concatenate([first, second], axis=0)
    return values


def all_shards(values):
    one = swap_with(values, "mp", 1)
    two = swap_with(values, "mp", 2)
    three = swap_with(two, "mp", 1)
    return [values, one, two, three]


def local(
    block_input,
    memory,
    cotangent,
    neighbour_table,
    requests,
    counts,
    neighbour_slots,
    memory_lengths,
    document_lengths,
    first_gain,
    first_bias,
    query_weight,
    key_weight,
    value_weight,
    position_weight,
    content_bias,
    position_bias,
    output_weight,
    second_gain,
    second_bias,
    inner_weight,
    inner_bias,
    outer_weight,
    outer_bias,
    gate_weight,
):
    model_index = lax.axis_index("mp").astype(jnp.int32)
    data_index = lax.axis_index("dp").astype(jnp.int32)
    data_size = lax.axis_size("dp")
    place = model_index.reshape(1)
    capacity = requests.shape[1]
    row = lambda v: v.reshape(1, -1)
    g1, b1, g2, b2 = row(first_gain), row(first_bias), row(second_gain), row(second_bias)

    def memory_of(k):
        return lax.dynamic_index_in_dim(memory, model_index ^ k, 0, keepdims=False)

    mem_blocks = [memory_of(0)] + [swap_with(memory_of(k), "mp", k) for k in (1, 2, 3)]

    if data_size <= 8:
        wanted = [lax.dynamic_index_in_dim(requests, data_index, 0, keepdims=False)]
        for k in range(1, data_size):
            mine = lax.dynamic_index_in_dim(requests, data_index ^ k, 0, keepdims=True)
            wanted.append(swap_with(mine, "dp", k)[0])
        found = jnp.take(neighbour_table, jnp.stack(wanted), axis=0, mode="clip")
        fetched = [found[0]] + [swap_with(found[k], "dp", k) for k in range(1, data_size)]
        slots = neighbour_slots ^ (data_index * capacity)
    else:
        wanted = lax.all_to_all(requests, "dp", split_axis=0, concat_axis=0, tiled=True)
        found = jnp.take(neighbour_table, wanted, axis=0, mode="clip")
        back = lax.all_to_all(found, "dp", split_axis=0, concat_axis=0, tiled=True)
        fetched = [back.reshape(data_size * capacity, D)]
        slots = neighbour_slots

    small = jnp.concatenate(
        [
            row(inner_bias.astype(F32)),
            jnp.concatenate([row(content_bias), row(position_bias)] * 2, axis=1),
        ],
        axis=0,
    )
    smalls = all_shards(small)
    wq, wk, wv, wp = (
        all_shards(w) for w in (query_weight, key_weight, value_weight, position_weight)
    )
    wo = all_shards(output_weight)
    wi = all_shards(inner_weight)
    wu = all_shards(outer_weight)
    table = position_table()

    (keys_in,) = call(
        norm_kernel, (shape((KEYS, D), BF16),), [place, block_input, *mem_blocks, g1, b1], smem=1
    )

    def attend(a, b):
        slot = lambda rows: shape((2, rows, SLOT), BF16)
        ins = [place, memory_lengths, document_lengths, keys_in, table]
        for w in (wq, wk, wv, wp, smalls):
            ins += [w[a], w[b]]
        return call(
            attend_kernel,
            (
                shape((4, SEG, KEYS), BF16),
                slot(SEG), slot(SEG), slot(KEYS), slot(KEYS), slot(KEYS), slot(SEG),
            ),
            ins,
            flops=2 * 10**10,
            scratch=[pltpu.VMEM((SEG, KEYS), F32)],
            smem=3,
        )

    saved_a = attend(0, 1)
    saved_b = attend(2, 3)
    att_a, att_b = saved_a[-1], saved_b[-1]

    square = shape((SEG, D), F32)
    middle, hidden, normed_middle, activation, slope = call(
        feed_kernel,
        (
            square, square, shape((SEG, D), BF16),
            shape((4, SEG, D), BF16), shape((4, SEG, D), BF16),
        ),
        [block_input, att_a, att_b, *wo, g2, b2, *wi, *smalls, *wu, row(outer_bias)],
        flops=6 * 10**9,
    )

    def mix_body(*refs):
        mix_kernel(len(fetched), *refs)

    mixed, grad_hidden, grad_gate = call(
        mix_body,
        (shape((SEG, D), BF16), square, shape((1, D), F32)),
        [place, document_lengths, *fetched, slots, cotangent, hidden, row(gate_weight)],
        flops=6 * 10**9,
        scratch=[pltpu.VMEM((capacity * requests.shape[0], D), BF16)],
        smem=2,
    )
    slot_grad = shape((2, SEG, SLOT), BF16)
    grad_middle, ga_a, ga_b, feed_pay = call(
        feed_back_kernel,
        (square, slot_grad, slot_grad, shape((4, FEED_ROWS, D), BF16)),
        [
            grad_hidden, grad_gate, middle, normed_middle, activation, slope, g2,
            att_a, att_b, *wo, *wi, *wu,
        ],
        flops=10**10,
    )

    pay_shape = shape((2, HEAD_ROWS, D), BF16)

    def back_far(*refs):
        attend_back_kernel(False, *refs)

    def back_near(*refs):
        attend_back_kernel(True, *refs)

    pay_far, grad_keys = call(
        back_far,
        (pay_shape, shape((KEYS, D), F32)),
        [
            keys_in, table, *saved_b[:-1], ga_b,
            wq[2], wq[3], wk[2], wk[3], wv[2], wv[3],
        ],
        flops=2 * 10**10,
    )
    ins = [
        keys_in, table, *saved_a[:-1], ga_a, wq[0], wq[1], wk[0], wk[1], wv[0], wv[1],
        grad_keys, grad_middle, block_input, *mem_blocks, place, g1,
    ]
    specs = [VMEM] * len(ins)
    specs[-2] = SMEM
    pay_near, input_grad = pl.pallas_call(
        back_near,
        out_shape=(pay_shape, square),
        in_specs=specs,
        out_specs=(VMEM, VMEM),
        scratch_shapes=[pltpu.VMEM((KEYS, D), F32)],
        compiler_params=pltpu.CompilerParams(vmem_limit_bytes=56 * 2**20),
        cost_estimate=pl.CostEstimate(flops=2 * 10**10, bytes_accessed=10**7, transcendentals=0),
    )(*ins)

    def to_owner(own, one, two, three):
        far = add_low(two, swap_with(three, "mp", 1))
        near = add_low(own, swap_with(one, "mp", 1))
        return add_low(near, swap_with(far, "mp", 2))

    feed_sum = sum_over(to_owner(*(feed_pay[k] for k in range(4))), "dp")
    tail = 4 * SLOT + 8
    far_0 = jnp.concatenate([pay_far[0, :tail], pay_near[0, tail:]], axis=0)
    far_1 = jnp.concatenate([pay_far[1, :tail], pay_near[1, tail:]], axis=0)
    head_sum = sum_over(to_owner(pay_near[0], pay_near[1], far_0, far_1), "dp")

    wide = head_sum.astype(F32)
    feed = feed_sum.astype(F32)
    vectors = feed[2 * D + SLOT :]
    return (
        mixed,
        input_grad,
        wide[tail],
        wide[tail + 1],
        wide[0:SLOT].T,
        wide[SLOT : 2 * SLOT].T,
        wide[2 * SLOT : 3 * SLOT].T,
        wide[3 * SLOT : 4 * SLOT].T,
        wide[4 * SLOT, :SLOT],
        wide[4 * SLOT, SLOT : 2 * SLOT],
        feed[2 * D : 2 * D + SLOT],
        vectors[1],
        vectors[2],
        feed[0:D],
        vectors[0],
        feed[D : 2 * D].T,
        vectors[3],
        vectors[4],
    )


def solution(mesh):
    return jax.shard_map(
        local,
        mesh=mesh,
        in_specs=(
            P(("dp", "mp"), None),
            P("dp", "mp", None),
            P(("dp", "mp"), None),
            P("dp", None),
            P(("dp", "mp"), None),
            P(("dp", "mp")),
            P(("dp", "mp"), None),
            P("dp"),
            P("dp"),
            P(),
            P(),
            P(None, "mp"),
            P(None, "mp"),
            P(None, "mp"),
            P(None, "mp"),
            P("mp"),
            P("mp"),
            P("mp", None),
            P(),
            P(),
            P(None, "mp"),
            P("mp"),
            P("mp", None),
            P(),
            P(),
        ),
        out_specs=(
            P(("dp", "mp"), None),
            P(("dp", "mp"), None),
            P(),
            P(),
            P(None, "mp"),
            P(None, "mp"),
            P(None, "mp"),
            P(None, "mp"),
            P("mp"),
            P("mp"),
            P("mp", None),
            P(),
            P(),
            P(None, "mp"),
            P("mp"),
            P("mp", None),
            P(),
            P(),
        ),
        check_vma=False,
    )
```

time: 994 us -> 334 us (0.34)
  local copies, waits for them, and re-layouts: 324 us -> 26.7 us
  waiting for transfers between devices: 341 us -> 123 us
  matrix products: 166 us -> 0 us
  Pallas kernels: 0 us -> 92.8 us
  blocking collectives: 65.9 us -> 0 us
  starting transfers between devices: 10.7 us -> 74 us
  other arithmetic: 49.7 us -> 13 us
  between operations: 15.3 us -> 1.52 us
  loops' own time: 12.1 us -> 0 us
    dot_general x70 -> x0, matrix products: 166 us -> none  [the longest x8 32.6 us: row_scores(): jnp.einsum('qhe,khe->hqk', split_heads(content_q), split_heads(key_rows),...]
    reshape x24 -> x0, local copies, waits for them, and re-layouts: 137 us -> none  [the longest x12 85.9 us: shift_rows(): folded = padded.reshape(leading + (KEYS + 1, SEG))[..., 1:, :]]
    ppermute x0 -> x59, waiting for transfers between devices: none -> 123 us  [swap_with(): return lax.ppermute(values, axis, [(i, i ^ k) for i in range(n)])]
    reduce_scatter x5 -> x0, waiting for transfers between devices: 105 us -> none  [the longest x1 44.6 us: local(): lax.psum_scatter(jnp.einsum('tf,df->td', grad_preact, inner_weight, prefe...]
    psum x1 -> x0, waiting for transfers between devices: 97.8 us -> none  [local(): lax.psum((grad_query_weight, grad_key_weight, grad_value_weight, grad_pos...]
    pallas_call x0 -> x8, Pallas kernels: none -> 92.8 us  [the longest x7 74.9 us: call(): pl.pallas_call(body, out_shape=outs, in_specs=[SMEM] * smem + [VMEM] * (l...]
    all_gather x5 -> x0, waiting for transfers between devices: 85.4 us -> none  [the longest x1 24.8 us: local(): lax.all_gather(normed_memory, 'mp', axis=1, tiled=True)]
    ppermute x0 -> x59, starting transfers between devices: none -> 74 us  [swap_with(): return lax.ppermute(values, axis, [(i, i ^ k) for i in range(n)])]
  transfers between devices with their start and end apart: 13 -> 59, of which waited for: 10 -> 18; matrix products, arithmetic and copies ran while one was open for 7% -> 9% of each run, Pallas kernels for 0% -> 21%
where the time goes in v1:
time: 334 us; the launch traced here: 331 us
  waiting for transfers between devices  123 us (37%)
  Pallas kernels  92.8 us (28%)
  starting transfers between devices  74 us (22%)
  local copies, waits for them, and re-layouts  26.7 us (8%)
  other arithmetic  13 us (4%)
    ppermute x59, waiting for transfers between devices, swap_with(): return lax.ppermute(values, axis, [(i, i ^ k) for i in range(n)])  123 us
    pallas_call x7, Pallas kernels, call(): pl.pallas_call(body, out_shape=outs, in_specs=[SMEM] * smem + [VMEM] * (l...  74.9 us
    ppermute x59, starting transfers between devices, swap_with(): return lax.ppermute(values, axis, [(i, i ^ k) for i in range(n)])  74 us
    pallas_call x1, Pallas kernels, local(): pl.pallas_call(back_near, out_shape=(pay_shape, square), in_specs=specs,...  17.9 us
    gather x1, local copies, waits for them, and re-layouts, local(): found = jnp.take(neighbour_table, jnp.stack(wanted), axis=0, mode='clip')  10.6 us
    convert_element_type x10, other arithmetic, add_low(): return sum((t.astype(F32) for t in terms)).astype(BF16)  7.29 us
    unnamed x85, local copies, waits for them, and re-layouts  7.24 us
  transfers between devices with their start and end apart: 59, of which 18 were waited for; matrix products, arithmetic and copies ran while one was open for 9% of the time, Pallas kernels for 21%

profile of v1, /device:TPU:0, one launch (start us, length us, event | category | flops | bytes accessed | tf_op | source)
XLA Modules:
  0.0 331.1 jit_solution(5100418939527438376)
XLA Ops:
  0.7 1.9 dynamic-slice_bitcast_fusion
  4.5 2.6 collective-permute-start.30
  8.1 1.6 collective-permute-start
  10.2 1.6 collective-permute-start.1
  11.7 2.5 collective-permute-start.2
  14.2 2.6 collective-permute-start.3
  16.8 2.9 collective-permute-start.4
  19.7 2.1 collective-permute-start.5
  22.2 3.9 %collective-permute-start.6 = (s32[1,256]{1,0:T(1,128)S(1)}, s32[1,256]{1,0:T(1,128)S(1)}, u32[]{:S(2)}, u32[]{:S(2)}) collective-permute-start(s32[1,256]{1,0:T(1,128)S(1)} %get-tuple-element.159), channel_id=1, source_target_pairs={{0,28},{4,24},{8,20},{12,16},{16,12},{20,8},{24,4},{28,0},{1,29},{... | collective-permute-start | bytes 3080 | tf_op jit(solution)/shard_map/ppermute | solution.py:365
  30.6 1.9 collective-permute-done.15.m2.refs_20_
  34.9 1.4 collective-permute-start.26
  37.4 10.6 %gather_fusion = bf16[2048,512]{1,0:T(8,128)(2,1)S(1)} fusion(bf16[4096,512]{1,0:T(8,128)(2,1)} %param.29, s32[2048]{0:T(1024)S(1)} %broadcast_clamp_fusion), kind=kCustom, calls=%fused_computation | custom fusion | bytes 4202496 | tf_op jit(solution)/shard_map/jit(_take)/gather | solution.py:448
  48.3 1.3 collective-permute-start.33
  51.2 3.1 shard_map.376.keys_ref.refs_0_
  55.0 1.5 collective-permute-start.39
  57.7 11.7 %shard_map.377 = (bf16[4,512,1024]{2,1,0:T(8,128)(2,1)}, bf16[2,512,128]{2,1,0:T(8,128)(2,1)}, bf16[2,512,128]{2,1,0:T(8,128)(2,1)}, bf16[2,1024,128]{2,1,0:T(8,...) custom-call(s32[1]{0:T(128)} %bitcast.place_ref.refs_0_.refs_22_, ...), custom_call_target="tpu_custom_call" | custom-call | flops 20000000000 | bytes 3153956 | tf_op jit(solution)/shard_map/pallas_call | solution.py:36
  70.2 9.6 %collective-permute-done.39.u2 = bf16[512,512]{1,0:T(8,128)(2,1)S(1)} collective-permute-done((bf16[512,512]{1,0:T(8,128)(2,1)S(1)}, bf16[512,512]{1,0:T(8,128)(2,1)S(1)}, u32[]{:S(2)}, u32[]{:S(2)}) %collective-permute-start.39) | collective-permute-done | bytes 524320 | tf_op jit(solution)/shard_map/ppermute | solution.py:365
  79.8 12.4 %shard_map.378 = (bf16[4,512,1024]{2,1,0:T(8,128)(2,1)}, bf16[2,512,128]{2,1,0:T(8,128)(2,1)}, bf16[2,512,128]{2,1,0:T(8,128)(2,1)}, bf16[2,1024,128]{2,1,0:T(8,...) custom-call(s32[1]{0:T(128)} %bitcast.place_ref.refs_0_.refs_22_, ...), custom_call_target="tpu_custom_call" | custom-call | flops 20000000000 | bytes 3153956 | tf_op jit(solution)/shard_map/pallas_call | solution.py:36
  92.4 3.6 %collective-permute-start.10 = (bf16[256,512]{1,0:T(8,128)(2,1)S(1)}, bf16[256,512]{1,0:T(8,128)(2,1)S(1)}, u32[]{:S(2)}, u32[]{:S(2)}) collective-permute-start(bf16[256,512]{1,0:T(8,128)(2,1)S(1)} %get-tuple-element.121), channel_id=1, source_target_pairs={{0,16},{4,20},{8,24},{12,28},{16,0},{20,4},{24,8},{28,12},{1,17},{... | collective-permute-start | bytes 786440 | tf_op jit(solution)/shard_map/ppermute | solution.py:365
  96.0 2.4 collective-permute-start.12
  98.5 2.4 collective-permute-start.13
  100.8 10.1 %shard_map.379 = (f32[512,512]{1,0:T(8,128)}, f32[512,512]{1,0:T(8,128)}, bf16[512,512]{1,0:T(8,128)(2,1)}, bf16[4,512,512]{2,1,0:T(8,128)(2,1)}, bf16[4,512,512]{2,1,0:T(8,128)(2,1)}) custom-call(bf16[512,512]{1,0:T(8,128)(2,1)} %refs_17_.1, bf16[2,512,128]{2,1,0:T(8,128)(2,1)} %get-tuple-element.48.att_a, bf16[2,512,128]{2,1,0:T(8,128)(2,1)} %get-tuple-element.49.att_b, ...), custom_call_target="tpu_custom_call" | custom-call | flops 6000000000 | bytes 5789696 | tf_op jit(solution)/shard_map/pallas_call | solution.py:36
  110.9 14.7 %collective-permute-done.10.refs_6_ = bf16[256,512]{1,0:T(8,128)(2,1)S(1)} collective-permute-done((bf16[256,512]{1,0:T(8,128)(2,1)S(1)}, bf16[256,512]{1,0:T(8,128)(2,1)S(1)}, u32[]{:S(2)}, u32[]{:S(2)}) %collective-permute-start.10) | collective-permute-done | bytes 262176 | tf_op jit(solution)/shard_map/ppermute | solution.py:365
  125.6 5.7 %collective-permute-done.11.refs_7_ = bf16[256,512]{1,0:T(8,128)(2,1)S(1)} collective-permute-done((bf16[256,512]{1,0:T(8,128)(2,1)S(1)}, bf16[256,512]{1,0:T(8,128)(2,1)S(1)}, u32[]{:S(2)}, u32[]{:S(2)}) %collective-permute-start.11) | collective-permute-done | bytes 262176 | tf_op jit(solution)/shard_map/ppermute | solution.py:365
  132.2 9.2 %shard_map.380 = (bf16[512,512]{1,0:T(8,128)(2,1)}, f32[512,512]{1,0:T(8,128)}, f32[1,512]{1,0:T(1,128)}) custom-call(s32[1]{0:T(128)} %bitcast.place_ref.refs_0_.refs_22_, s32[4]{0:T(128)} %refs_1_.1, bf16[256,512]{1,0:T(8,128)(2,1)} %get-tuple-element.125.refs_2_, bf16[256,512]{1,0:T(8,128)(2,1)} %copy-done.14, bf16[256,512]{1,0:T(8,128)(2,1)} %copy-done.15, ...), custom_call_target="tpu_custom_call" | custom-call | flops 6000000000 | bytes 3680276 | tf_op jit(solution)/shard_map/pallas_call | solution.py:36
  141.3 12.7 %shard_map.381 = (f32[512,512]{1,0:T(8,128)}, bf16[2,512,128]{2,1,0:T(8,128)(2,1)}, bf16[2,512,128]{2,1,0:T(8,128)(2,1)}, bf16[4,1216,512]{2,1,0:T(8,128)(2,1)}) custom-call(f32[512,512]{1,0:T(8,128)} %get-tuple-element.58.gh_ref, f32[1,512]{1,0:T(1,128)} %get-tuple-element.59.gate_grad_ref, f32[512,512]{1,0:T(8,128)} %get-tuple-element.60.middle_ref, ...), custom_call_target="tpu_custom_call" | custom-call | flops 10000000000 | bytes 12062720 | tf_op jit(solution)/shard_map/pallas_call | solution.py:36
  154.0 1.8 slice_bitcast_fusion.1
  155.9 15.8 %shard_map.382 = (bf16[2,576,512]{2,1,0:T(8,128)(2,1)}, f32[1024,512]{1,0:T(8,128)}) custom-call(bf16[1024,512]{1,0:T(8,128)(2,1)} %shard_map.376.keys_ref.refs_0_, bf16[1024,512]{1,0:T(8,128)(2,1)} %constant.137.table_ref.refs_1_, bf16[4,512,1024]{2,1,0:T(8,128)(2,1)} %get-tuple-element.65.refs_2_, bf16[2,512,128]{2,1,0:T(8,128)(2,1)} %get-tuple-element.66.refs_3_, ...), custom_call_target="tpu_custom_call" | custom-call | flops 20000000000 | bytes 9437184 | tf_op jit(solution)/shard_map/pallas_call | solution.py:36
  171.8 17.9 %shard_map.383 = (bf16[2,576,512]{2,1,0:T(8,128)(2,1)}, f32[512,512]{1,0:T(8,128)}) custom-call(bf16[1024,512]{1,0:T(8,128)(2,1)} %shard_map.376.keys_ref.refs_0_, bf16[1024,512]{1,0:T(8,128)(2,1)} %constant.137.table_ref.refs_1_, bf16[4,512,1024]{2,1,0:T(8,128)(2,1)} %get-tuple-element.52.refs_2_, bf16[2,512,128]{2,1,0:T(8,128)(2,1)} %get-tuple-element.53.refs_3_, ...), custom_call_target="tpu_custom_call" | custom-call | flops 20000000000 | bytes 10000000 | tf_op jit(solution)/shard_map/pallas_call | solution.py:555
  193.1 2.7 fusion
  198.1 40.5 %collective-permute-done.43 = bf16[576,512]{1,0:T(8,128)(2,1)} collective-permute-done((bf16[576,512]{1,0:T(8,128)(2,1)S(1)}, bf16[576,512]{1,0:T(8,128)(2,1)}, u32[]{:S(2)}, u32[]{:S(2)}) %collective-permute-start.43) | collective-permute-done | bytes 589856 | tf_op jit(solution)/shard_map/ppermute | solution.py:365
  238.5 1.5 add_convert_fusion.2
  240.0 1.5 collective-permute-start.44
  241.5 2.6 add_convert_fusion
  244.8 5.2 %collective-permute-done.44 = bf16[288,512]{1,0:T(8,128)(2,1)S(1)} collective-permute-done((bf16[288,512]{1,0:T(8,128)(2,1)S(1)}, bf16[288,512]{1,0:T(8,128)(2,1)S(1)}, u32[]{:S(2)}, u32[]{:S(2)}) %collective-permute-start.44) | collective-permute-done | bytes 294944 | tf_op jit(solution)/shard_map/ppermute | solution.py:365
  250.1 11.0 %collective-permute-start.45 = (bf16[144,512]{1,0:T(8,128)(2,1)S(1)}, bf16[144,512]{1,0:T(8,128)(2,1)S(1)}, u32[]{:S(2)}, u32[]{:S(2)}) collective-permute-start(bf16[144,512]{1,0:T(8,128)(2,1)S(1)} %constant_dynamic-slice_fusion.4), channel_id=1, source_target_pairs={{0,8},{4,12},{8,0},{12,4},{16,24},{20,28},{24,16},{28,20},{1,9},{5... | collective-permute-start | bytes 442376 | tf_op jit(solution)/shard_map/ppermute | solution.py:365
  261.1 3.1 collective-permute-done.45
  264.5 8.8 %collective-permute-start.54 = (bf16[304,512]{1,0:T(8,128)(2,1)S(1)}, bf16[304,512]{1,0:T(8,128)(2,1)S(1)}, u32[]{:S(2)}, u32[]{:S(2)}) collective-permute-start(bf16[304,512]{1,0:T(8,128)(2,1)S(1)} %constant_dynamic-slice_fusion.1), channel_id=1, source_target_pairs={{0,8},{4,12},{8,0},{12,4},{16,24},{20,28},{24,16},{28,20},{1,9},{5... | collective-permute-start | bytes 933896 | tf_op jit(solution)/shard_map/ppermute | solution.py:365
  274.4 6.1 %collective-permute-done.46 = bf16[72,512]{1,0:T(8,128)(2,1)S(1)} collective-permute-done((bf16[72,512]{1,0:T(8,128)(2,1)S(1)}, bf16[72,512]{1,0:T(8,128)(2,1)S(1)}, u32[]{:S(2)}, u32[]{:S(2)}) %collective-permute-start.46) | collective-permute-done | bytes 73760 | tf_op jit(solution)/shard_map/ppermute | solution.py:365
  280.4 3.4 %collective-permute-start.47 = (bf16[72,512]{1,0:T(8,128)(2,1)S(1)}, bf16[72,512]{1,0:T(8,128)(2,1)S(1)}, u32[]{:S(2)}, u32[]{:S(2)}) collective-permute-start(bf16[72,512]{1,0:T(8,128)(2,1)S(1)} %add_convert_fusion.8), channel_id=1, source_target_pairs={{0,16},{4,20},{8,24},{12,28},{16,0},{20,4},{24,8},{28,12},{1,17},{... | collective-permute-start | bytes 221192 | tf_op jit(solution)/shard_map/ppermute | solution.py:365
  284.1 5.1 %collective-permute-done.47 = bf16[72,512]{1,0:T(8,128)(2,1)S(1)} collective-permute-done((bf16[72,512]{1,0:T(8,128)(2,1)S(1)}, bf16[72,512]{1,0:T(8,128)(2,1)S(1)}, u32[]{:S(2)}, u32[]{:S(2)}) %collective-permute-start.47) | collective-permute-done | bytes 73760 | tf_op jit(solution)/shard_map/ppermute | solution.py:365
  290.3 3.4 %collective-permute-done.55 = bf16[152,512]{1,0:T(8,128)(2,1)S(1)} collective-permute-done((bf16[152,512]{1,0:T(8,128)(2,1)S(1)}, bf16[152,512]{1,0:T(8,128)(2,1)S(1)}, u32[]{:S(2)}, u32[]{:S(2)}) %collective-permute-start.55) | collective-permute-done | bytes 155680 | tf_op jit(solution)/shard_map/ppermute | solution.py:365
  293.8 1.4 collective-permute-done.48
  296.1 5.8 %collective-permute-done.56 = bf16[152,512]{1,0:T(8,128)(2,1)S(1)} collective-permute-done((bf16[152,512]{1,0:T(8,128)(2,1)S(1)}, bf16[152,512]{1,0:T(8,128)(2,1)S(1)}, u32[]{:S(2)}, u32[]{:S(2)}) %collective-permute-start.56) | collective-permute-done | bytes 155680 | tf_op jit(solution)/shard_map/ppermute | solution.py:365
  302.2 9.1 %collective-permute-done.57 = bf16[304,512]{1,0:T(8,128)(2,1)S(1)} collective-permute-done((bf16[304,512]{1,0:T(8,128)(2,1)S(1)}, bf16[304,512]{1,0:T(8,128)(2,1)S(1)}, u32[]{:S(2)}, u32[]{:S(2)}) %collective-permute-start.57) | collective-permute-done | bytes 311328 | tf_op jit(solution)/shard_map/ppermute | solution.py:365
  311.4 1.6 collective-permute-start.58
  317.6 8.9 %collective-permute-done.58 = bf16[608,512]{1,0:T(8,128)(2,1)S(1)} collective-permute-done((bf16[608,512]{1,0:T(8,128)(2,1)S(1)}, bf16[608,512]{1,0:T(8,128)(2,1)S(1)}, u32[]{:S(2)}, u32[]{:S(2)}) %collective-permute-start.58) | collective-permute-done | bytes 622624 | tf_op jit(solution)/shard_map/ppermute | solution.py:365
  329.6 1.3 copy.55
  (211 shorter events, 35.7 us)
Async XLA Ops:
  2.6 26.7 %collective-permute-start.14 = (bf16[128,512]{1,0:T(8,128)(2,1)S(1)}, bf16[128,512]{1,0:T(8,128)(2,1)S(1)}, u32[]{:S(2)}, u32[]{:S(2)}) collective-permute-start(bf16[128,512]{1,0:T(8,128)(2,1)S(1)} %get-tuple-element.150), channel_id=1, source_target_pairs={{0,1},{1,0},{2,3},{3,2},{4,5},{5,4},{6,7},{7,6},{8,9},{9,8},{10,11... | collective-permute-start | bytes 393224 | tf_op jit(solution)/shard_map/ppermute | solution.py:365
  9.7 18.8 %collective-permute-start.21 = (f32[2,512]{1,0:T(2,128)S(1)}, f32[2,512]{1,0:T(2,128)S(1)}, u32[]{:S(2)}, u32[]{:S(2)}) collective-permute-start(f32[2,512]{1,0:T(2,128)S(1)} %maximum_maximum_fusion.s0), channel_id=1, source_target_pairs={{0,1},{1,0},{2,3},{3,2},{4,5},{5,4},{6,7},{7,6},{8,9},{9,8},{10,11... | collective-permute-start | bytes 12296 | tf_op jit(solution)/shard_map/ppermute | solution.py:365
  9.7 19.6 %collective-permute-start.31 = (f32[2,512]{1,0:T(2,128)S(1)}, f32[2,512]{1,0:T(2,128)S(1)}, u32[]{:S(2)}, u32[]{:S(2)}) collective-permute-start(f32[2,512]{1,0:T(2,128)S(1)} %collective-permute-done.30.s0.s2), channel_id=1, source_target_pairs={{0,1},{1,0},{2,3},{3,2},{4,5},{5,4},{6,7},{7,6},{8,9},{9,8},{10,11... | collective-permute-start | bytes 12296 | tf_op jit(solution)/shard_map/ppermute | solution.py:365
  19.7 7.2 %collective-permute-start.5 = (s32[1,256]{1,0:T(1,128)S(1)}, s32[1,256]{1,0:T(1,128)S(1)}, u32[]{:S(2)}, u32[]{:S(2)}) collective-permute-start(s32[1,256]{1,0:T(1,128)S(1)} %get-tuple-element.166), channel_id=1, source_target_pairs={{0,24},{4,28},{8,16},{12,20},{16,8},{20,12},{24,0},{28,4},{1,25},{... | collective-permute-start | bytes 3080 | tf_op jit(solution)/shard_map/ppermute | solution.py:365
  22.2 6.3 %collective-permute-start.6 = (s32[1,256]{1,0:T(1,128)S(1)}, s32[1,256]{1,0:T(1,128)S(1)}, u32[]{:S(2)}, u32[]{:S(2)}) collective-permute-start(s32[1,256]{1,0:T(1,128)S(1)} %get-tuple-element.159), channel_id=1, source_target_pairs={{0,28},{4,24},{8,20},{12,16},{16,12},{20,8},{24,4},{28,0},{1,29},{... | collective-permute-start | bytes 3080 | tf_op jit(solution)/shard_map/ppermute | solution.py:365
  28.5 6.4 %collective-permute-start.17 = (bf16[512,128]{1,0:T(8,128)(2,1)S(1)}, bf16[512,128]{1,0:T(8,128)(2,1)S(1)}, u32[]{:S(2)}, u32[]{:S(2)}) collective-permute-start(bf16[512,128]{1,0:T(8,128)(2,1)S(1)} %copy-done.23), channel_id=1, source_target_pairs={{0,1},{1,0},{2,3},{3,2},{4,5},{5,4},{6,7},{7,6},{8,9},{9,8},{10,11... | collective-permute-start | bytes 393224 | tf_op jit(solution)/shard_map/ppermute | solution.py:365
  29.2 7.0 %collective-permute-start.18 = (bf16[512,128]{1,0:T(8,128)(2,1)S(1)}, bf16[512,128]{1,0:T(8,128)(2,1)S(1)}, u32[]{:S(2)}, u32[]{:S(2)}) collective-permute-start(bf16[512,128]{1,0:T(8,128)(2,1)S(1)} %copy-done.24), channel_id=1, source_target_pairs={{0,1},{1,0},{2,3},{3,2},{4,5},{5,4},{6,7},{7,6},{8,9},{9,8},{10,11... | collective-permute-start | bytes 393224 | tf_op jit(solution)/shard_map/ppermute | solution.py:365
  29.3 7.4 %collective-permute-start.19 = (bf16[512,128]{1,0:T(8,128)(2,1)S(1)}, bf16[512,128]{1,0:T(8,128)(2,1)S(1)}, u32[]{:S(2)}, u32[]{:S(2)}) collective-permute-start(bf16[512,128]{1,0:T(8,128)(2,1)S(1)} %copy-done.25), channel_id=1, source_target_pairs={{0,1},{1,0},{2,3},{3,2},{4,5},{5,4},{6,7},{7,6},{8,9},{9,8},{10,11... | collective-permute-start | bytes 393224 | tf_op jit(solution)/shard_map/ppermute | solution.py:365
  32.5 15.8 %collective-permute-start.22 = (bf16[512,128]{1,0:T(8,128)(2,1)S(1)}, bf16[512,128]{1,0:T(8,128)(2,1)}, u32[]{:S(2)}, u32[]{:S(2)}) collective-permute-start(bf16[512,128]{1,0:T(8,128)(2,1)S(1)} %copy-done.23), channel_id=1, source_target_pairs={{0,2},{1,3},{2,0},{3,1},{4,6},{5,7},{6,4},{7,5},{8,10},{9,11},{10,... | collective-permute-start | bytes 393224 | tf_op jit(solution)/shard_map/ppermute | solution.py:365
  34.2 15.4 %collective-permute-start.24 = (bf16[512,128]{1,0:T(8,128)(2,1)S(1)}, bf16[512,128]{1,0:T(8,128)(2,1)}, u32[]{:S(2)}, u32[]{:S(2)}) collective-permute-start(bf16[512,128]{1,0:T(8,128)(2,1)S(1)} %copy-done.24), channel_id=1, source_target_pairs={{0,2},{1,3},{2,0},{3,1},{4,6},{5,7},{6,4},{7,5},{8,10},{9,11},{10,... | collective-permute-start | bytes 393224 | tf_op jit(solution)/shard_map/ppermute | solution.py:365
  34.9 14.9 %collective-permute-start.26 = (bf16[512,128]{1,0:T(8,128)(2,1)S(1)}, bf16[512,128]{1,0:T(8,128)(2,1)}, u32[]{:S(2)}, u32[]{:S(2)}) collective-permute-start(bf16[512,128]{1,0:T(8,128)(2,1)S(1)} %copy-done.25), channel_id=1, source_target_pairs={{0,2},{1,3},{2,0},{3,1},{4,6},{5,7},{6,4},{7,5},{8,10},{9,11},{10,... | collective-permute-start | bytes 393224 | tf_op jit(solution)/shard_map/ppermute | solution.py:365
  36.3 11.8 %collective-permute-start.20 = (bf16[512,128]{1,0:T(8,128)(2,1)S(1)}, bf16[512,128]{1,0:T(8,128)(2,1)}, u32[]{:S(2)}, u32[]{:S(2)}) collective-permute-start(bf16[512,128]{1,0:T(8,128)(2,1)S(1)} %copy-done.21), channel_id=1, source_target_pairs={{0,1},{1,0},{2,3},{3,2},{4,5},{5,4},{6,7},{7,6},{8,9},{9,8},{10,11... | collective-permute-start | bytes 393224 | tf_op jit(solution)/shard_map/ppermute | solution.py:365
  36.7 13.4 %collective-permute-start.28 = (bf16[512,128]{1,0:T(8,128)(2,1)S(1)}, bf16[512,128]{1,0:T(8,128)(2,1)}, u32[]{:S(2)}, u32[]{:S(2)}) collective-permute-start(bf16[512,128]{1,0:T(8,128)(2,1)S(1)} %copy-done.21), channel_id=1, source_target_pairs={{0,2},{1,3},{2,0},{3,1},{4,6},{5,7},{6,4},{7,5},{8,10},{9,11},{10,... | collective-permute-start | bytes 393224 | tf_op jit(solution)/shard_map/ppermute | solution.py:365
  48.1 6.2 %collective-permute-start.32 = (bf16[128,512]{1,0:T(8,128)(2,1)S(1)}, bf16[128,512]{1,0:T(8,128)(2,1)S(1)}, u32[]{:S(2)}, u32[]{:S(2)}) collective-permute-start(bf16[128,512]{1,0:T(8,128)(2,1)S(1)} %copy-done.22), channel_id=1, source_target_pairs={{0,1},{1,0},{2,3},{3,2},{4,5},{5,4},{6,7},{7,6},{8,9},{9,8},{10,11... | collective-permute-start | bytes 393224 | tf_op jit(solution)/shard_map/ppermute | solution.py:365
  48.3 6.7 %collective-permute-start.33 = (bf16[128,512]{1,0:T(8,128)(2,1)S(1)}, bf16[128,512]{1,0:T(8,128)(2,1)S(1)}, u32[]{:S(2)}, u32[]{:S(2)}) collective-permute-start(bf16[128,512]{1,0:T(8,128)(2,1)S(1)} %copy-done.22), channel_id=1, source_target_pairs={{0,2},{1,3},{2,0},{3,1},{4,6},{5,7},{6,4},{7,5},{8,10},{9,11},{10,... | collective-permute-start | bytes 393224 | tf_op jit(solution)/shard_map/ppermute | solution.py:365
  49.6 6.8 %collective-permute-start.23 = (bf16[512,128]{1,0:T(8,128)(2,1)}, bf16[512,128]{1,0:T(8,128)(2,1)S(1)}, u32[]{:S(2)}, u32[]{:S(2)}) collective-permute-start(bf16[512,128]{1,0:T(8,128)(2,1)} %collective-permute-done.22.q0.refs_9_), channel_id=1, source_target_pairs={{0,1},{1,0},{2,3},{3,2},{4,5},{5,4},{6,7},{7,6},{8,9},{9,8},{10,11... | collective-permute-start | bytes 393224 | tf_op jit(solution)/shard_map/ppermute | solution.py:365
  49.8 7.3 %collective-permute-start.25 = (bf16[512,128]{1,0:T(8,128)(2,1)}, bf16[512,128]{1,0:T(8,128)(2,1)S(1)}, u32[]{:S(2)}, u32[]{:S(2)}) collective-permute-start(bf16[512,128]{1,0:T(8,128)(2,1)} %collective-permute-done.24.k0.refs_11_), channel_id=1, source_target_pairs={{0,1},{1,0},{2,3},{3,2},{4,5},{5,4},{6,7},{7,6},{8,9},{9,8},{10,11... | collective-permute-start | bytes 393224 | tf_op jit(solution)/shard_map/ppermute | solution.py:365
  50.2 7.0 %collective-permute-start.27 = (bf16[512,128]{1,0:T(8,128)(2,1)}, bf16[512,128]{1,0:T(8,128)(2,1)S(1)}, u32[]{:S(2)}, u32[]{:S(2)}) collective-permute-start(bf16[512,128]{1,0:T(8,128)(2,1)} %collective-permute-done.26.v0.refs_13_), channel_id=1, source_target_pairs={{0,1},{1,0},{2,3},{3,2},{4,5},{5,4},{6,7},{7,6},{8,9},{9,8},{10,11... | collective-permute-start | bytes 393224 | tf_op jit(solution)/shard_map/ppermute | solution.py:365
  54.3 15.7 %collective-permute-start.36 = (bf16[512,512]{1,0:T(8,128)(2,1)S(1)}, bf16[512,512]{1,0:T(8,128)(2,1)S(1)}, u32[]{:S(2)}, u32[]{:S(2)}) collective-permute-start(bf16[512,512]{1,0:T(8,128)(2,1)S(1)} %copy-done.6), channel_id=1, source_target_pairs={{0,2},{1,3},{2,0},{3,1},{4,6},{5,7},{6,4},{7,5},{8,10},{9,11},{10,... | collective-permute-start | bytes 1572872 | tf_op jit(solution)/shard_map/ppermute | solution.py:365
  55.0 24.8 %collective-permute-start.39 = (bf16[512,512]{1,0:T(8,128)(2,1)S(1)}, bf16[512,512]{1,0:T(8,128)(2,1)S(1)}, u32[]{:S(2)}, u32[]{:S(2)}) collective-permute-start(bf16[512,512]{1,0:T(8,128)(2,1)S(1)} %copy-done.7), channel_id=1, source_target_pairs={{0,2},{1,3},{2,0},{3,1},{4,6},{5,7},{6,4},{7,5},{8,10},{9,11},{10,... | collective-permute-start | bytes 1572872 | tf_op jit(solution)/shard_map/ppermute | solution.py:365
  56.5 13.6 %collective-permute-start.7 = (bf16[256,512]{1,0:T(8,128)(2,1)S(1)}, bf16[256,512]{1,0:T(8,128)(2,1)S(1)}, u32[]{:S(2)}, u32[]{:S(2)}) collective-permute-start(bf16[256,512]{1,0:T(8,128)(2,1)S(1)} %get-tuple-element.124), channel_id=1, source_target_pairs={{0,4},{4,0},{8,12},{12,8},{16,20},{20,16},{24,28},{28,24},{1,5},{5... | collective-permute-start | bytes 786440 | tf_op jit(solution)/shard_map/ppermute | solution.py:365
  57.1 12.3 %collective-permute-start.29 = (bf16[512,128]{1,0:T(8,128)(2,1)}, bf16[512,128]{1,0:T(8,128)(2,1)S(1)}, u32[]{:S(2)}, u32[]{:S(2)}) collective-permute-start(bf16[512,128]{1,0:T(8,128)(2,1)} %collective-permute-done.28.p0), channel_id=1, source_target_pairs={{0,1},{1,0},{2,3},{3,2},{4,5},{5,4},{6,7},{7,6},{8,9},{9,8},{10,11... | collective-permute-start | bytes 393224 | tf_op jit(solution)/shard_map/ppermute | solution.py:365
  57.2 12.4 %collective-permute-start.34 = (bf16[128,512]{1,0:T(8,128)(2,1)S(1)}, bf16[128,512]{1,0:T(8,128)(2,1)S(1)}, u32[]{:S(2)}, u32[]{:S(2)}) collective-permute-start(bf16[128,512]{1,0:T(8,128)(2,1)S(1)} %collective-permute-done.33.o2), channel_id=1, source_target_pairs={{0,1},{1,0},{2,3},{3,2},{4,5},{5,4},{6,7},{7,6},{8,9},{9,8},{10,11... | collective-permute-start | bytes 393224 | tf_op jit(solution)/shard_map/ppermute | solution.py:365
  69.5 22.9 %collective-permute-start.35 = (bf16[512,512]{1,0:T(8,128)(2,1)S(1)}, bf16[512,512]{1,0:T(8,128)(2,1)S(1)}, u32[]{:S(2)}, u32[]{:S(2)}) collective-permute-start(bf16[512,512]{1,0:T(8,128)(2,1)S(1)} %copy-done.6), channel_id=1, source_target_pairs={{0,1},{1,0},{2,3},{3,2},{4,5},{5,4},{6,7},{7,6},{8,9},{9,8},{10,11... | collective-permute-start | bytes 1572872 | tf_op jit(solution)/shard_map/ppermute | solution.py:365
  69.6 26.4 %collective-permute-start.38 = (bf16[512,512]{1,0:T(8,128)(2,1)S(1)}, bf16[512,512]{1,0:T(8,128)(2,1)S(1)}, u32[]{:S(2)}, u32[]{:S(2)}) collective-permute-start(bf16[512,512]{1,0:T(8,128)(2,1)S(1)} %copy-done.7), channel_id=1, source_target_pairs={{0,1},{1,0},{2,3},{3,2},{4,5},{5,4},{6,7},{7,6},{8,9},{9,8},{10,11... | collective-permute-start | bytes 1572872 | tf_op jit(solution)/shard_map/ppermute | solution.py:365
  70.0 22.2 %collective-permute-start.8 = (bf16[256,512]{1,0:T(8,128)(2,1)S(1)}, bf16[256,512]{1,0:T(8,128)(2,1)S(1)}, u32[]{:S(2)}, u32[]{:S(2)}) collective-permute-start(bf16[256,512]{1,0:T(8,128)(2,1)S(1)} %get-tuple-element.123), channel_id=1, source_target_pairs={{0,8},{4,12},{8,0},{12,4},{16,24},{20,28},{24,16},{28,20},{1,9},{5... | collective-permute-start | bytes 786440 | tf_op jit(solution)/shard_map/ppermute | solution.py:365
  70.1 26.0 %collective-permute-start.37 = (bf16[512,512]{1,0:T(8,128)(2,1)S(1)}, bf16[512,512]{1,0:T(8,128)(2,1)S(1)}, u32[]{:S(2)}, u32[]{:S(2)}) collective-permute-start(bf16[512,512]{1,0:T(8,128)(2,1)S(1)} %collective-permute-done.36.i2), channel_id=1, source_target_pairs={{0,1},{1,0},{2,3},{3,2},{4,5},{5,4},{6,7},{7,6},{8,9},{9,8},{10,11... | collective-permute-start | bytes 1572872 | tf_op jit(solution)/shard_map/ppermute | solution.py:365
  79.8 18.6 %collective-permute-start.40 = (bf16[512,512]{1,0:T(8,128)(2,1)S(1)}, bf16[512,512]{1,0:T(8,128)(2,1)S(1)}, u32[]{:S(2)}, u32[]{:S(2)}) collective-permute-start(bf16[512,512]{1,0:T(8,128)(2,1)S(1)} %collective-permute-done.39.u2), channel_id=1, source_target_pairs={{0,1},{1,0},{2,3},{3,2},{4,5},{5,4},{6,7},{7,6},{8,9},{9,8},{10,11... | collective-permute-start | bytes 1572872 | tf_op jit(solution)/shard_map/ppermute | solution.py:365
  92.3 18.6 %collective-permute-start.9 = (bf16[256,512]{1,0:T(8,128)(2,1)S(1)}, bf16[256,512]{1,0:T(8,128)(2,1)S(1)}, u32[]{:S(2)}, u32[]{:S(2)}) collective-permute-start(bf16[256,512]{1,0:T(8,128)(2,1)S(1)} %get-tuple-element.122), channel_id=1, source_target_pairs={{0,12},{4,8},{8,4},{12,0},{16,28},{20,24},{24,20},{28,16},{1,13},{... | collective-permute-start | bytes 786440 | tf_op jit(solution)/shard_map/ppermute | solution.py:365
  92.4 33.2 %collective-permute-start.10 = (bf16[256,512]{1,0:T(8,128)(2,1)S(1)}, bf16[256,512]{1,0:T(8,128)(2,1)S(1)}, u32[]{:S(2)}, u32[]{:S(2)}) collective-permute-start(bf16[256,512]{1,0:T(8,128)(2,1)S(1)} %get-tuple-element.121), channel_id=1, source_target_pairs={{0,16},{4,20},{8,24},{12,28},{16,0},{20,4},{24,8},{28,12},{1,17},{... | collective-permute-start | bytes 786440 | tf_op jit(solution)/shard_map/ppermute | solution.py:365
  96.0 35.3 %collective-permute-start.11 = (bf16[256,512]{1,0:T(8,128)(2,1)S(1)}, bf16[256,512]{1,0:T(8,128)(2,1)S(1)}, u32[]{:S(2)}, u32[]{:S(2)}) collective-permute-start(bf16[256,512]{1,0:T(8,128)(2,1)S(1)} %get-tuple-element.120), channel_id=1, source_target_pairs={{0,20},{4,16},{8,28},{12,24},{16,4},{20,0},{24,12},{28,8},{1,21},{... | collective-permute-start | bytes 786440 | tf_op jit(solution)/shard_map/ppermute | solution.py:365
  96.0 35.2 %collective-permute-start.12 = (bf16[256,512]{1,0:T(8,128)(2,1)S(1)}, bf16[256,512]{1,0:T(8,128)(2,1)S(1)}, u32[]{:S(2)}, u32[]{:S(2)}) collective-permute-start(bf16[256,512]{1,0:T(8,128)(2,1)S(1)} %get-tuple-element.119), channel_id=1, source_target_pairs={{0,24},{4,28},{8,16},{12,20},{16,8},{20,12},{24,0},{28,4},{1,25},{... | collective-permute-start | bytes 786440 | tf_op jit(solution)/shard_map/ppermute | solution.py:365
  98.5 32.8 %collective-permute-start.13 = (bf16[256,512]{1,0:T(8,128)(2,1)S(1)}, bf16[256,512]{1,0:T(8,128)(2,1)S(1)}, u32[]{:S(2)}, u32[]{:S(2)}) collective-permute-start(bf16[256,512]{1,0:T(8,128)(2,1)S(1)} %get-tuple-element.118), channel_id=1, source_target_pairs={{0,28},{4,24},{8,20},{12,16},{16,12},{20,8},{24,4},{28,0},{1,29},{... | collective-permute-start | bytes 786440 | tf_op jit(solution)/shard_map/ppermute | solution.py:365
  155.8 37.3 %collective-permute-start.51 = (bf16[1216,512]{1,0:T(8,128)(2,1)S(1)}, bf16[1216,512]{1,0:T(8,128)(2,1)S(1)}, u32[]{:S(2)}, u32[]{:S(2)}) collective-permute-start(bf16[1216,512]{1,0:T(8,128)(2,1)S(1)} %get-tuple-element.115), channel_id=1, source_target_pairs={{0,1},{1,0},{2,3},{3,2},{4,5},{5,4},{6,7},{7,6},{8,9},{9,8},{10,11... | collective-permute-start | bytes 3735560 | tf_op jit(solution)/shard_map/ppermute | solution.py:365
  193.1 48.4 %collective-permute-start.50 = (bf16[1216,512]{1,0:T(8,128)(2,1)S(1)}, bf16[1216,512]{1,0:T(8,128)(2,1)}, u32[]{:S(2)}, u32[]{:S(2)}) collective-permute-start(bf16[1216,512]{1,0:T(8,128)(2,1)S(1)} %get-tuple-element.114), channel_id=1, source_target_pairs={{0,1},{1,0},{2,3},{3,2},{4,5},{5,4},{6,7},{7,6},{8,9},{9,8},{10,11... | collective-permute-start | bytes 3735560 | tf_op jit(solution)/shard_map/ppermute | solution.py:365
  195.8 45.7 %collective-permute-start.52 = (bf16[1216,512]{1,0:T(8,128)(2,1)}, bf16[1216,512]{1,0:T(8,128)(2,1)}, u32[]{:S(2)}, u32[]{:S(2)}) collective-permute-start(bf16[1216,512]{1,0:T(8,128)(2,1)} %fusion), channel_id=1, source_target_pairs={{0,2},{1,3},{2,0},{3,1},{4,6},{5,7},{6,4},{7,5},{8,10},{9,11},{10,... | collective-permute-start | bytes 3735560 | tf_op jit(solution)/shard_map/ppermute | solution.py:365
  197.0 41.5 %collective-permute-start.43 = (bf16[576,512]{1,0:T(8,128)(2,1)S(1)}, bf16[576,512]{1,0:T(8,128)(2,1)}, u32[]{:S(2)}, u32[]{:S(2)}) collective-permute-start(bf16[576,512]{1,0:T(8,128)(2,1)S(1)} %add_convert_fusion.3), channel_id=1, source_target_pairs={{0,2},{1,3},{2,0},{3,1},{4,6},{5,7},{6,4},{7,5},{8,10},{9,11},{10,... | collective-permute-start | bytes 1769480 | tf_op jit(solution)/shard_map/ppermute | solution.py:365
  240.0 10.0 %collective-permute-start.44 = (bf16[288,512]{1,0:T(8,128)(2,1)S(1)}, bf16[288,512]{1,0:T(8,128)(2,1)S(1)}, u32[]{:S(2)}, u32[]{:S(2)}) collective-permute-start(bf16[288,512]{1,0:T(8,128)(2,1)S(1)} %constant_dynamic-slice_fusion.5), channel_id=1, source_target_pairs={{0,4},{4,0},{8,12},{12,8},{16,20},{20,16},{24,28},{28,24},{1,5},{5... | collective-permute-start | bytes 884744 | tf_op jit(solution)/shard_map/ppermute | solution.py:365
  244.1 20.1 %collective-permute-start.53 = (bf16[608,512]{1,0:T(8,128)(2,1)S(1)}, bf16[608,512]{1,0:T(8,128)(2,1)S(1)}, u32[]{:S(2)}, u32[]{:S(2)}) collective-permute-start(bf16[608,512]{1,0:T(8,128)(2,1)S(1)} %constant_dynamic-slice_fusion.2), channel_id=1, source_target_pairs={{0,4},{4,0},{8,12},{12,8},{16,20},{20,16},{24,28},{28,24},{1,5},{5... | collective-permute-start | bytes 1867784 | tf_op jit(solution)/shard_map/ppermute | solution.py:365
  250.1 14.1 %collective-permute-start.45 = (bf16[144,512]{1,0:T(8,128)(2,1)S(1)}, bf16[144,512]{1,0:T(8,128)(2,1)S(1)}, u32[]{:S(2)}, u32[]{:S(2)}) collective-permute-start(bf16[144,512]{1,0:T(8,128)(2,1)S(1)} %constant_dynamic-slice_fusion.4), channel_id=1, source_target_pairs={{0,8},{4,12},{8,0},{12,4},{16,24},{20,28},{24,16},{28,20},{1,9},{5... | collective-permute-start | bytes 442376 | tf_op jit(solution)/shard_map/ppermute | solution.py:365
  264.5 19.4 %collective-permute-start.54 = (bf16[304,512]{1,0:T(8,128)(2,1)S(1)}, bf16[304,512]{1,0:T(8,128)(2,1)S(1)}, u32[]{:S(2)}, u32[]{:S(2)}) collective-permute-start(bf16[304,512]{1,0:T(8,128)(2,1)S(1)} %constant_dynamic-slice_fusion.1), channel_id=1, source_target_pairs={{0,8},{4,12},{8,0},{12,4},{16,24},{20,28},{24,16},{28,20},{1,9},{5... | collective-permute-start | bytes 933896 | tf_op jit(solution)/shard_map/ppermute | solution.py:365
  273.2 7.2 %collective-permute-start.46 = (bf16[72,512]{1,0:T(8,128)(2,1)S(1)}, bf16[72,512]{1,0:T(8,128)(2,1)S(1)}, u32[]{:S(2)}, u32[]{:S(2)}) collective-permute-start(bf16[72,512]{1,0:T(8,128)(2,1)S(1)} %constant_dynamic-slice_fusion.3), channel_id=1, source_target_pairs={{0,16},{4,20},{8,24},{12,28},{16,0},{20,4},{24,8},{28,12},{1,17},{... | collective-permute-start | bytes 221192 | tf_op jit(solution)/shard_map/ppermute | solution.py:365
  280.4 8.8 %collective-permute-start.47 = (bf16[72,512]{1,0:T(8,128)(2,1)S(1)}, bf16[72,512]{1,0:T(8,128)(2,1)S(1)}, u32[]{:S(2)}, u32[]{:S(2)}) collective-permute-start(bf16[72,512]{1,0:T(8,128)(2,1)S(1)} %add_convert_fusion.8), channel_id=1, source_target_pairs={{0,16},{4,20},{8,24},{12,28},{16,0},{20,4},{24,8},{28,12},{1,17},{... | collective-permute-start | bytes 221192 | tf_op jit(solution)/shard_map/ppermute | solution.py:365
  284.0 9.6 %collective-permute-start.55 = (bf16[152,512]{1,0:T(8,128)(2,1)S(1)}, bf16[152,512]{1,0:T(8,128)(2,1)S(1)}, u32[]{:S(2)}, u32[]{:S(2)}) collective-permute-start(bf16[152,512]{1,0:T(8,128)(2,1)S(1)} %constant_dynamic-slice_fusion), channel_id=1, source_target_pairs={{0,16},{4,20},{8,24},{12,28},{16,0},{20,4},{24,8},{28,12},{1,17},{... | collective-permute-start | bytes 466952 | tf_op jit(solution)/shard_map/ppermute | solution.py:365
  293.7 8.1 %collective-permute-start.56 = (bf16[152,512]{1,0:T(8,128)(2,1)S(1)}, bf16[152,512]{1,0:T(8,128)(2,1)S(1)}, u32[]{:S(2)}, u32[]{:S(2)}) collective-permute-start(bf16[152,512]{1,0:T(8,128)(2,1)S(1)} %add_convert_fusion.6), channel_id=1, source_target_pairs={{0,16},{4,20},{8,24},{12,28},{16,0},{20,4},{24,8},{28,12},{1,17},{... | collective-permute-start | bytes 466952 | tf_op jit(solution)/shard_map/ppermute | solution.py:365
  295.3 6.8 %collective-permute-start.49 = (bf16[288,512]{1,0:T(8,128)(2,1)S(1)}, bf16[288,512]{1,0:T(8,128)(2,1)S(1)}, u32[]{:S(2)}, u32[]{:S(2)}) collective-permute-start(bf16[288,512]{1,0:T(8,128)(2,1)S(1)} %pad_maximum_fusion.3), channel_id=1, source_target_pairs={{0,4},{4,0},{8,12},{12,8},{16,20},{20,16},{24,28},{28,24},{1,5},{5... | collective-permute-start | bytes 884744 | tf_op jit(solution)/shard_map/ppermute | solution.py:365
  301.9 9.3 %collective-permute-start.57 = (bf16[304,512]{1,0:T(8,128)(2,1)S(1)}, bf16[304,512]{1,0:T(8,128)(2,1)S(1)}, u32[]{:S(2)}, u32[]{:S(2)}) collective-permute-start(bf16[304,512]{1,0:T(8,128)(2,1)S(1)} %pad_maximum_fusion.2), channel_id=1, source_target_pairs={{0,8},{4,12},{8,0},{12,4},{16,24},{20,28},{24,16},{28,20},{1,9},{5... | collective-permute-start | bytes 933896 | tf_op jit(solution)/shard_map/ppermute | solution.py:365
  311.4 15.2 %collective-permute-start.58 = (bf16[608,512]{1,0:T(8,128)(2,1)S(1)}, bf16[608,512]{1,0:T(8,128)(2,1)S(1)}, u32[]{:S(2)}, u32[]{:S(2)}) collective-permute-start(bf16[608,512]{1,0:T(8,128)(2,1)S(1)} %pad_maximum_fusion), channel_id=1, source_target_pairs={{0,4},{4,0},{8,12},{12,8},{16,20},{20,16},{24,28},{28,24},{1,5},{5... | collective-permute-start | bytes 1867784 | tf_op jit(solution)/shard_map/ppermute | solution.py:365
  (50 other events, 633.7 us)
